TPU v7x, 128 devices: a whole 4x4x4 slice. The times are simulated.
128 devices in a mesh: group: 8 (over x, y_hi), shard: 16 (over z, y_lo, core).
Axes of the slice: x: 4, y: 4 (y_hi: 2, y_lo: 2; y = y_hi * 2 + y_lo), z: 4, core: 2. Of those that a mesh axis runs over, the one named last changes fastest.
Arguments:
- images: bfloat16 [128, 28, 28, 512], P(('group', 'shard')), may hold values from -6 to 6
- cotangent: bfloat16 [128, 28, 28, 512], P(('group', 'shard')), may hold values from -6 to 6
- dw_kernel: bfloat16 [49, 512], P(None, 'shard'), may hold values from -0.875 to 0.875
- norm_gain: float32 [512], replicated, may hold values from 0.1 to 1.9
- w_up: bfloat16 [512, 2048], P('shard'), may hold values from -0.25 to 0.25
- w_down: bfloat16 [2048, 512], P('shard'), may hold values from -0.125 to 0.125
- owner_table: int32 [8], replicated, may hold values from 0 to 7, each once
Outputs:
- mixed: bfloat16 [128, 28, 28, 512], P(('group', 'shard'))
- back_images: bfloat16 [128, 28, 28, 512], P(('group', 'shard'))
- statistics: float32 [8, 2, 512, 512], P('group')
Inputs may be any that keep to these rules, and one draw needn't show every extreme that they name: `owner_table`: each of 0 to 7 stands once.
All inputs are finite; a program needn't handle non-finite values.
Results may differ from a plain program's by a relative error of at most 0.014.
Values may be sent and summed in bfloat16 or wider, within the bound.
A program may use at most 128 MiB of HBM per device.

v0:
```python
import jax
import jax.numpy as jnp
from jax import lax
from jax.sharding import PartitionSpec as P

BLK = 512


def normed_map(xfloat, kernel, gain):
    width = xfloat.shape[-1]
    taps = kernel.astype(jnp.float32).reshape(7, 7, 1, width)
    conv = lax.conv_general_dilated(
        xfloat,
        taps,
        (1, 1),
        "SAME",
        dimension_numbers=("NHWC", "HWIO", "NHWC"),
        feature_group_count=width,
        precision=lax.Precision.HIGHEST,
    )
    mean = jnp.mean(conv, axis=-1, keepdims=True)
    var = jnp.mean((conv - mean) ** 2, axis=-1, keepdims=True)
    return (conv - mean) / jnp.sqrt(var + 1e-06) * gain


def normal_cdf(v):
    return 0.5 * (1.0 + lax.erf(v * 0.7071067811865476))


def normal_pdf(v):
    return 0.3989422804014327 * jnp.exp(-0.5 * v * v)


def tiles_of(matrix, size):
    rows, cols = matrix.shape
    return (
        matrix.reshape(rows // size, size, cols // size, size)
        .transpose(0, 2, 1, 3)
        .reshape(-1, size, size)
    )


def local(images, cotangent, dw_kernel, norm_gain, w_up, w_down, owner_table):
    kernel, up_full, down_full = (
        lax.all_gather(dw_kernel, "shard", axis=1, tiled=True),
        lax.all_gather(w_up, "shard", axis=0, tiled=True),
        lax.all_gather(w_down, "shard", axis=0, tiled=True),
    )
    width = images.shape[-1]
    xfloat = images.astype(jnp.float32)
    normed, pullback = jax.vjp(lambda v: normed_map(v, kernel, norm_gain), xfloat)
    u = normed.astype(jnp.bfloat16).reshape(-1, width)
    pre = jnp.dot(u, up_full, preferred_element_type=jnp.float32)
    act = (pre * normal_cdf(pre)).astype(jnp.bfloat16)
    branch = jnp.dot(act, down_full, preferred_element_type=jnp.float32)
    mixed = (xfloat + branch.reshape(images.shape)).astype(jnp.bfloat16)
    back_rows = cotangent.reshape(-1, width)
    back_act = lax.dot_general(
        back_rows, down_full, (((1,), (1,)), ((), ())), preferred_element_type=jnp.float32
    )
    back_pre = (back_act * (normal_cdf(pre) + pre * normal_pdf(pre))).astype(jnp.bfloat16)
    back_u = lax.dot_general(
        back_pre, up_full, (((1,), (1,)), ((), ())), preferred_element_type=jnp.float32
    )
    back_x = pullback(back_u.reshape(images.shape))[0]
    back_images = (cotangent.astype(jnp.float32) + back_x).astype(jnp.bfloat16)
    group_rows = u.shape[0] * lax.axis_size("shard")
    scale = 1.0 / jnp.sqrt(jnp.float32(group_rows))
    part_up = (
        lax.dot_general(u, back_pre, (((0,), (0,)), ((), ())), preferred_element_type=jnp.float32)
        * scale
    )
    part_down = (
        lax.dot_general(
            act, back_rows, (((0,), (0,)), ((), ())), preferred_element_type=jnp.float32
        )
        * scale
    )
    grad_up, grad_down = (
        lax.psum(part_up.astype(jnp.bfloat16), "shard").astype(jnp.float32),
        lax.psum(part_down.astype(jnp.bfloat16), "shard").astype(jnp.float32),
    )
    blocks = jnp.concatenate([tiles_of(grad_up, BLK), tiles_of(grad_down, BLK)], axis=0)
    ordered = jnp.take(blocks, owner_table, axis=0)
    left = jnp.einsum("kij,klj->kil", ordered, ordered, precision=lax.Precision.HIGHEST) / BLK
    right = jnp.einsum("kji,kjl->kil", ordered, ordered, precision=lax.Precision.HIGHEST) / BLK
    statistics = lax.psum_scatter(
        jnp.stack([left, right], axis=1).astype(jnp.bfloat16),
        "group",
        scatter_dimension=0,
        tiled=True,
    ).astype(jnp.float32)
    return (mixed, back_images, statistics)


def solution(mesh):
    return jax.shard_map(
        local,
        mesh=mesh,
        in_specs=(
            P(("group", "shard"), None, None, None),
            P(("group", "shard"), None, None, None),
            P(None, "shard"),
            P(),
            P("shard", None),
            P("shard", None),
            P(),
        ),
        out_specs=(
            P(("group", "shard"), None, None, None),
            P(("group", "shard"), None, None, None),
            P("group", None, None, None),
        ),
        check_vma=False,
    )
```

profile of v0, /device:TPU:5, one launch (start us, length us, event | category | flops | bytes accessed | tf_op | source)
XLA Modules:
  0.0 671.4 jit_solution(7995794684557257392)
XLA Ops:
  7.2 0.0 all-gather.3.cloned.1.call-start
  7.2 0.7 all-gather.3.cloned.1.call-update
  7.9 0.0 all-gather.5.cloned.1.call-start
  7.9 0.7 all-gather.5.cloned.1.call-update
  8.6 0.0 all-reduce.7.cloned.1.call-start
  8.7 22.2 %all_gather.9 = bf16[49,512]{0,1:T(8,128)(2,1)S(1)} all-gather(bf16[49,32]{0,1:T(8,128)(2,1)} %param.9), channel_id=1, replica_groups=mesh['group'=8,'shard'=16] {'shard'}, dimensions={1}, use_global_device_ids=true | all-gather | bytes 53312 | tf_op jit(solution)/shard_map/all_gather | solution.py:45
  30.9 0.1 copy.30
  31.1 0.0 copy-start.3
  31.1 26.0 %fusion.34 = (f32[28,28]{1,0:T(8,128)S(1)}, f32[1,28,28,512]{3,0,2,1:T(1,128)S(1)}) fusion(bf16[7,7,1,512]{3,2,1,0:T(2,128)(2,1)S(1)} %reshape.161, bf16[1,28,28,512]{3,2,1,0:T(8,128)(2,1)} %param.7), kind=kOutput, calls=%fused_computation.60 | convolution fusion | flops 35069168 | bytes 2461760 | tf_op jit(solution)/shard_map/jvp()/conv_general_dilated | solution.py:12
  57.1 0.2 reshape.147
  57.3 11.6 %multiply_reduce_fusion.1 = f32[28,28]{1,0:T(8,128)S(1)} fusion(f32[1,28,28,512]{3,0,2,1:T(1,128)S(1)} %get-tuple-element.17, f32[28,28]{1,0:T(8,128)S(1)} %broadcast_multiply_fusion), kind=kLoop, calls=%fused_computation.38 | loop fusion | flops 1203440 | bytes 1611904 | tf_op jit(solution)/shard_map/jvp()/reduce_sum | solution.py:22
  68.9 20.9 %convert_reduce_fusion = bf16[28,28,512]{2,1,0:T(8,128)(2,1)S(1)} fusion(f32[512]{0:T(512)S(1)} %copy-done.6, f32[28,28]{1,0:T(8,128)S(1)} %get-tuple-element.15, f32[1,28,28,512]{3,0,2,1:T(1,128)S(1)} %get-tuple-element.17, f32[28,28]{1,0:T(8,128)S(1)} %broadcast_multiply_fusion), kind=kLoop, calls=%fused_computation.37 | loop fusion | flops 1605632 | bytes 2416768 | tf_op jit(solution)/shard_map/convert_element_type | solution.py:52
  89.8 1.0 reshape.145
  90.9 5.4 multiply_convert_fusion.2
  96.3 1.7 copy-done.10
  98.0 3.7 multiply_convert_fusion.3
  101.7 6.4 fusion.9
  108.1 1.7 copy-done.9
  109.8 3.7 multiply_convert_fusion.4
  113.5 4.5 reshape.150
  118.0 3.3 copy.53
  121.3 0.0 all-reduce.7.cloned.1.call-update
  121.4 0.0 all-reduce.5.cloned.1.call-start
  121.4 0.6 copy-done.7
  122.0 132.8 %all-reduce.7.cloned.1.call-done = (bf16[4,512,512]{2,1,0:T(8,128)(2,1)}, bf16[4,512,512]{2,1,0:T(8,128)(2,1)}) async-done(((bf16[4,512,512]{2,1,0:T(8,128)(2,1)}, bf16[4,512,512]{2,1,0:T(8,128)(2,1)}), (bf16[4,512,512]{2,1,0:T(8,128)(2,1)}, bf16[4,512,512]{2,1,0:T(8,128)(2,1)})) %all-reduce.7.cloned.1.call-update) | async-done | bytes 4194320 | tf_op jit(solution)/shard_map/psum | solution.py:81
  254.8 6.0 maximum_convert_fusion
  260.8 7.7 %gather_fusion = f32[8,512,512]{2,1,0:T(8,128)} fusion(f32[8,512,512]{2,1,0:T(8,128)} %maximum_convert_fusion, s32[1024]{0:T(1024)S(1)} %pad_clamp_fusion), kind=kCustom, calls=%fused_computation | custom fusion | bytes 16777248 | tf_op jit(solution)/shard_map/jit(_take)/gather | solution.py:84
  268.5 21.1 %fusion.11 = bf16[8,1,512,512]{3,2,0,1:T(8,128)(2,1)S(1)} fusion(f32[8,512,512]{2,1,0:T(8,128)} %gather_fusion, pred[8]{0:T(512)(128)(4,1)S(1)} %compare_and_fusion), kind=kOutput, calls=%fused_computation.18 | convolution fusion | flops 12891193344 | bytes 12582920 | tf_op jit(solution)/shard_map/kji,kjl->kil/dot_general | solution.py:86
  289.6 15.9 %fusion.10 = bf16[8,1,512,512]{3,2,0,1:T(8,128)(2,1)} fusion(f32[8,512,512]{2,1,0:T(8,128)S(1)} %copy-done, pred[8]{0:T(512)(128)(4,1)S(1)} %compare_and_fusion), kind=kOutput, calls=%fused_computation.17 | convolution fusion | flops 12891193344 | bytes 12582920 | tf_op jit(solution)/shard_map/kij,klj->kil/dot_general | solution.py:85
  305.6 6.2 pad_maximum_fusion
  311.8 0.0 all-reduce.5.cloned.1.call-update
  311.8 0.1 sqrt.21
  311.9 0.5 copy-done.8
  312.4 0.6 dynamic-slice
  313.1 5.6 fusion.24
  318.6 0.1 neg.16
  318.7 4.4 fusion.35
  323.1 1.4 reshape.146
  324.5 3.4 reshape.148
  328.0 12.3 %multiply_reduce_fusion = f32[28,28]{1,0:T(8,128)S(1)} fusion(f32[1,28,28,512]{3,0,2,1:T(1,128)S(1)} %reshape.148, f32[28,28]{1,0:T(8,128)S(1)} %get-tuple-element.14, f32[512]{0:T(512)S(1)} %copy-done.6, f32[1,28,28,512]{3,0,2,1:T(1,128)S(1)} %get-tuple-element.17, f32[28,28]{1,0:T(8,128)S(1)} %broadcast_multiply_fusion), kind=kLoop, calls=%fused_computation.36 | loop fusion | flops 2006256 | bytes 3222720 | tf_op jit(solution)/shard_map/transpose(jvp())/reduce_sum | solution.py:23
  340.3 12.2 %multiply_reduce_fusion.2 = f32[28,28]{1,0:T(8,128)S(1)} fusion(f32[28,28]{1,0:T(8,128)S(1)} %multiply_multiply_fusion.1, f32[1,28,28,512]{3,0,2,1:T(1,128)S(1)} %get-tuple-element.17, f32[28,28]{1,0:T(8,128)S(1)} %broadcast_multiply_fusion), kind=kLoop, calls=%fused_computation.41 | loop fusion | flops 1203440 | bytes 1615040 | tf_op jit(solution)/shard_map/transpose(jvp())/reduce_sum | solution.py:22
  352.6 4.1 fusion.53
  356.7 22.5 %fusion.20 = bf16[1,28,28,512]{3,0,2,1:T(2,128)(2,1)S(1)} fusion(bf16[7,7,512,1]{2,3,1,0:T(2,128)(2,1)S(1)} %reshape.162, bf16[1,28,28,512]{3,2,1,0:T(8,128)(2,1)S(1)} %copy-done.4, f32[1,28,28,512]{3,0,2,1:T(1,128)S(1)} %fusion.53), kind=kOutput, calls=%fused_computation.27 | convolution fusion | flops 209215488 | bytes 3261440 | tf_op jit(solution)/shard_map/transpose(jvp())/conv_general_dilated | solution.py:12
  379.2 1.2 copy.38
  380.4 0.7 copy-done.1
  381.0 1.3 add_convert_fusion
  382.3 278.6 %all-reduce.5.cloned.1.call-done = bf16[8,2,512,512]{3,2,0,1:T(8,128)(2,1)} async-done(((bf16[8,2,512,512]{3,2,0,1:T(8,128)(2,1)}), bf16[8,2,512,512]{3,2,0,1:T(8,128)(2,1)}) %all-reduce.5.cloned.1.call-update) | async-done | bytes 8388624
  660.9 3.5 bitcast_convert_fusion
  (28 shorter events, 0.2 us)
Async XLA Ops:
  7.2 83.7 %all-gather.3.cloned.1.call-start = ((), (), s32[]{:S(2)}) async-start(), calls=%async_computation | async-start | bytes 2228224 | tf_op jit(solution)/shard_map/all_gather | solution.py:46
  7.9 93.8 %all-gather.5.cloned.1.call-start = ((), (), s32[]{:S(2)}) async-start(), calls=%async_computation.1 | async-start | bytes 2228224 | tf_op jit(solution)/shard_map/all_gather | solution.py:47
  8.6 246.2 %all-reduce.7.cloned.1.call-start = ((), (), s32[]{:S(2)}) async-start(), calls=%async_computation.3 | async-start | bytes 8388608 | tf_op jit(solution)/shard_map/psum | solution.py:81
  31.1 26.0 %copy-start.3 = (bf16[1,28,28,512]{3,2,1,0:T(8,128)(2,1)S(1)}, bf16[1,28,28,512]{3,2,1,0:T(8,128)(2,1)}, u32[]{:S(2)}) copy-start(bf16[1,28,28,512]{3,2,1,0:T(8,128)(2,1)} %param.8) | copy-start | bytes 2408452
  57.1 11.9 %copy-start.6 = (f32[512]{0:T(512)S(1)}, f32[512]{0:T(512)}, u32[]{:S(2)}) copy-start(f32[512]{0:T(512)} %param.10) | copy-start | bytes 6148
  96.3 1.7 copy-start.10
  101.7 8.1 %copy-start.5 = (bf16[784,512]{1,0:T(8,128)(2,1)S(1)}, bf16[784,512]{1,0:T(8,128)(2,1)}, u32[]{:S(2)}) copy-start(bf16[784,512]{1,0:T(8,128)(2,1)} %reshape.145) | copy-start | bytes 2408452
  108.1 1.7 copy-start.9
  121.3 0.7 copy-start.7
  121.4 539.5 %all-reduce.5.cloned.1.call-start = ((), (), s32[]{:S(2)}) async-start(), calls=%async_computation.2 | async-start | bytes 16777216
  268.5 21.1 %copy-start = (f32[8,512,512]{2,1,0:T(8,128)S(1)}, f32[8,512,512]{2,1,0:T(8,128)}, u32[]{:S(2)}) copy-start(f32[8,512,512]{2,1,0:T(8,128)} %gather_fusion) | copy-start | bytes 25165828
  311.8 0.7 copy-start.8
  352.6 4.1 copy-start.4
  356.7 23.7 %copy-start.2 = (bf16[1,28,28,512]{3,2,1,0:T(8,128)(2,1)S(1)}, bf16[1,28,28,512]{3,2,1,0:T(8,128)(2,1)}, u32[]{:S(2)}) copy-start(bf16[1,28,28,512]{3,2,1,0:T(8,128)(2,1)} %param.7) | copy-start | bytes 2408452
  379.2 1.9 copy-start.1
Sparse Core Ops, SparseCore 0:
  9.7 36.8 all-gather.2
  48.3 34.0 all-gather.4
  121.5 133.3 all-reduce.6
  311.9 348.9 all-reduce.4
where the time goes:
time: 680 us; the launch traced here: 671 us
  waiting for transfers between devices  413 us (61%)
  matrix products  115 us (17%)
  other arithmetic  78.1 us (11%)
  local copies, waits for them, and re-layouts  28.9 us (4%)
  blocking collectives  22.2 us (3%)
  between operations  14.4 us (2%)
    unnamed x5, waiting for transfers between devices  280 us
    psum x1, waiting for transfers between devices, local(): lax.psum(part_down.astype(jnp.bfloat16), 'shard').astype(jnp.float32)  133 us
    conv_general_dilated x2, matrix products, normed_map(): lax.conv_general_dilated(xfloat, taps, (1, 1), 'SAME', dimension_numbers=...  48.5 us
    reduce_sum x2, other arithmetic, normed_map(): var = jnp.mean((conv - mean) ** 2, axis=-1, keepdims=True)  23.8 us
    all_gather x1, blocking collectives, local(): lax.all_gather(dw_kernel, 'shard', axis=1, tiled=True)  22.2 us
    dot_general x1, matrix products, local(): jnp.einsum('kji,kjl->kil', ordered, ordered, precision=lax.Precision.HIGH...  21.1 us
    convert_element_type x1, other arithmetic, local(): u = normed.astype(jnp.bfloat16).reshape(-1, width)  20.9 us
    dot_general x1, matrix products, local(): jnp.einsum('kij,klj->kil', ordered, ordered, precision=lax.Precision.HIGH...  15.9 us
  transfers between devices with their start and end apart: 4, of which 2 were waited for; matrix products, arithmetic and copies ran while one was open for 21% of the time, Pallas kernels for 0%

commit v1 on v0

--- a/solution.py
+++ b/solution.py
@@ -1,6 +1,10 @@
+import functools
+
 import jax
 import jax.numpy as jnp
 from jax import lax
+from jax.experimental import pallas as pl
+from jax.experimental.pallas import tpu as pltpu
 from jax.sharding import PartitionSpec as P
 
 BLK = 512
@@ -40,6 +44,146 @@
     )
 
 
+MESH = pl.DeviceIdType.MESH
+
+
+def stats_kernel(n, tile, p_ref, out_ref, a0, q, a1, gfull, m, c1, ag, a0s, a0r, a1s, a1r, gs, gr, cs, cr, ds, dr, es, er, fs, fr):
+    g, s = lax.axis_index("group"), lax.axis_index("shard")
+    core, pair = lax.rem(s, 2), lax.div(s, 2)
+    sib = s + 1 - 2 * core
+    half, chunk = tile // 2, tile // n
+    f32, bf16 = jnp.float32, jnp.bfloat16
+
+    def dma(src, dst, ssem, rsem, group, shard):
+        return pltpu.make_async_remote_copy(
+            src_ref=src, dst_ref=dst, send_sem=ssem, recv_sem=rsem, device_id=(group, shard), device_id_type=MESH
+        )
+
+    target = (pair, 2 * lax.rem(g + 1, n) + core)
+    source = (lax.rem(pair + n - 1, n), 2 * g + core)
+    barrier = pltpu.get_barrier_semaphore()
+
+    def greet(group, shard):
+        pl.semaphore_signal(barrier, inc=1, device_id=(group, shard), device_id_type=MESH)
+
+    greet(g, sib)
+    for i in range(1, n):
+        greet(g, 2 * lax.rem(pair + i, n) + core)
+        greet(lax.rem(g + i, n), s)
+    greet(*target)
+    greet(*source)
+    pl.semaphore_wait(barrier, 2 * n + 1)
+
+    own = pl.ds(pl.multiple_of(core * half, half), half)
+    other = pl.ds(pl.multiple_of((1 - core) * half, half), half)
+
+    def slot(i):
+        return lax.rem(pair + 1 + i, n)
+
+    def a0_copy(i):
+        return dma(p_ref.at[slot(i), other], a0.at[i], a0s.at[i], a0r.at[i], g, sib)
+
+    def a1_copy(i):
+        return dma(q.at[i], a1.at[i], a1s.at[i], a1r.at[i], g, 2 * slot(i) + core)
+
+    @pl.loop(0, n)
+    def _(i):
+        a0_copy(i).start()
+
+    @pl.loop(0, n - 1)
+    def _(i):
+        a0_copy(i).wait_recv()
+        q[i] = (p_ref[slot(i), own].astype(f32) + a0[i].astype(f32)).astype(bf16)
+        a1_copy(i).start()
+
+    a0_copy(n - 1).wait_recv()
+    acc = p_ref[pair, own].astype(f32) + a0[n - 1].astype(f32)
+    for i in range(n - 1):
+        a1_copy(i).wait_recv()
+        acc = acc + a1[i].astype(f32)
+    gfull[own] = acc.astype(bf16)
+    g_copy = dma(gfull.at[own], gfull.at[own], gs, gr, g, sib)
+    g_copy.start()
+    g_copy.wait_recv()
+    whole = gfull[...]
+    side = jnp.where(core == 0, whole, whole.T)
+    stat = lax.dot_general(side, side, (((1,), (1,)), ((), ())), preferred_element_type=f32)
+    m[...] = (stat * (1.0 / tile)).astype(bf16).reshape(n, chunk, tile)
+
+    def c_copy(i):
+        j = lax.rem(g + i, n)
+        return dma(m.at[j], c1.at[i], cs.at[i], cr.at[i], j, s)
+
+    for i in range(1, n):
+        c_copy(i).start()
+    acc = m[g].astype(f32)
+    for i in range(1, n):
+        c_copy(i).wait_recv()
+        acc = acc + c1[i].astype(f32)
+    c1[0] = acc.astype(bf16)
+    d_copy = dma(c1.at[0], ag.at[target[1]], ds, dr, *target)
+    d_copy.start()
+    dma(c1.at[0], ag.at[s], ds, dr, *target).wait_recv()
+
+    def e_copy(i):
+        return dma(ag.at[s], ag.at[s], es.at[i], er.at[i], g, 2 * lax.rem(pair + i, n) + core)
+
+    def f_copy(i):
+        j = 2 * lax.rem(pair + n - i, n) + core
+        return dma(ag.at[j], ag.at[j], fs.at[i], fr.at[i], g, sib)
+
+    for i in range(1, n):
+        e_copy(i).start()
+    f_copy(0).start()
+    for i in range(1, n):
+        e_copy(i).wait_recv()
+        f_copy(i).start()
+    for i in range(n):
+        f_copy(i).wait_recv()
+    for k in range(2 * n):
+        out_ref[k % 2, pl.ds((k // 2 + n - 1) % n * chunk, chunk)] = ag[k].astype(f32)
+
+    for i in range(n):
+        a0_copy(i).wait_send()
+        f_copy(i).wait_send()
+    for i in range(n - 1):
+        a1_copy(i).wait_send()
+        c_copy(i + 1).wait_send()
+        e_copy(i + 1).wait_send()
+    g_copy.wait_send()
+    d_copy.wait_send()
+
+
+def group_statistics(parts, n):
+    tile = parts.shape[-1]
+    half, chunk = tile // 2, tile // n
+    bf16 = jnp.bfloat16
+    dma_sem = pltpu.SemaphoreType.DMA
+    return pl.pallas_call(
+        functools.partial(stats_kernel, n, tile),
+        out_shape=jax.ShapeDtypeStruct((2, tile, tile), jnp.float32),
+        in_specs=[pl.BlockSpec(memory_space=pltpu.VMEM)],
+        out_specs=pl.BlockSpec(memory_space=pltpu.VMEM),
+        scratch_shapes=[
+            pltpu.VMEM((n, half, tile), bf16),
+            pltpu.VMEM((n - 1, half, tile), bf16),
+            pltpu.VMEM((n - 1, half, tile), bf16),
+            pltpu.VMEM((tile, tile), bf16),
+            pltpu.VMEM((n, chunk, tile), bf16),
+            pltpu.VMEM((n, chunk, tile), bf16),
+            pltpu.VMEM((2 * n, chunk, tile), bf16),
+            dma_sem((n,)), dma_sem((n,)),
+            dma_sem((n - 1,)), dma_sem((n - 1,)),
+            dma_sem, dma_sem,
+            dma_sem((n,)), dma_sem((n,)),
+            dma_sem, dma_sem,
+            dma_sem((n,)), dma_sem((n,)),
+            dma_sem((n,)), dma_sem((n,)),
+        ],
+        compiler_params=pltpu.CompilerParams(collective_id=0, has_side_effects=True, vmem_limit_bytes=40 * 2**20),
+    )(parts)
+
+
 def local(images, cotangent, dw_kernel, norm_gain, w_up, w_down, owner_table):
     kernel, up_full, down_full = (
         lax.all_gather(dw_kernel, "shard", axis=1, tiled=True),
@@ -76,20 +220,11 @@
         )
         * scale
     )
-    grad_up, grad_down = (
-        lax.psum(part_up.astype(jnp.bfloat16), "shard").astype(jnp.float32),
-        lax.psum(part_down.astype(jnp.bfloat16), "shard").astype(jnp.float32),
-    )
-    blocks = jnp.concatenate([tiles_of(grad_up, BLK), tiles_of(grad_down, BLK)], axis=0)
+    blocks = jnp.concatenate(
+        [tiles_of(part_up.astype(jnp.bfloat16), BLK), tiles_of(part_down.astype(jnp.bfloat16), BLK)], axis=0
+    )
     ordered = jnp.take(blocks, owner_table, axis=0)
-    left = jnp.einsum("kij,klj->kil", ordered, ordered, precision=lax.Precision.HIGHEST) / BLK
-    right = jnp.einsum("kji,kjl->kil", ordered, ordered, precision=lax.Precision.HIGHEST) / BLK
-    statistics = lax.psum_scatter(
-        jnp.stack([left, right], axis=1).astype(jnp.bfloat16),
-        "group",
-        scatter_dimension=0,
-        tiled=True,
-    ).astype(jnp.float32)
+    statistics = group_statistics(ordered, lax.axis_size("group"))[None]
     return (mixed, back_images, statistics)
 
 

time: 680 us -> 271 us (0.40)
  the two profiles are of different devices: /device:TPU:5 before, /device:TPU:1 now
where the time goes in v1:
time: 271 us; the launch traced here: 270 us
  matrix products  78.3 us (29%)
  other arithmetic  70.2 us (26%)
  Pallas kernels  58.7 us (22%)
  local copies, waits for them, and re-layouts  23.9 us (9%)
  blocking collectives  23.1 us (9%)
  between operations  14.3 us (5%)
    pallas_call x1, Pallas kernels, group_statistics(): pl.pallas_call(functools.partial(stats_kernel, n, tile), out_shape=jax.Sh...  58.7 us
    conv_general_dilated x2, matrix products, normed_map(): lax.conv_general_dilated(xfloat, taps, (1, 1), 'SAME', dimension_numbers=...  48.5 us
    reduce_sum x2, other arithmetic, normed_map(): var = jnp.mean((conv - mean) ** 2, axis=-1, keepdims=True)  23.8 us
    all_gather x1, blocking collectives, local(): lax.all_gather(dw_kernel, 'shard', axis=1, tiled=True)  23.1 us
    convert_element_type x1, other arithmetic, local(): u = normed.astype(jnp.bfloat16).reshape(-1, width)  20.9 us
    reduce_sum x1, other arithmetic, normed_map(): return (conv - mean) / jnp.sqrt(var + 1e-06) * gain  13.6 us
    unnamed x28, local copies, waits for them, and re-layouts  7.08 us
    dot_general x1, matrix products, local(): lax.dot_general(back_rows, down_full, (((1,), (1,)), ((), ())), preferred...  6.2 us
  transfers between devices with their start and end apart: 2, of which 0 were waited for; matrix products, arithmetic and copies ran while one was open for 26% of the time, Pallas kernels for 0%

profile of v1, /device:TPU:1, one launch (start us, length us, event | category | flops | bytes accessed | tf_op | source)
XLA Modules:
  0.0 270.0 jit_solution(15423545253893973873)
XLA Ops:
  7.2 0.0 all-gather.3.cloned.1.call-start
  7.2 0.7 all-gather.3.cloned.1.call-update
  7.9 0.0 all-gather.5.cloned.1.call-start
  7.9 0.7 all-gather.5.cloned.1.call-update
  8.6 23.1 %all_gather.9 = bf16[49,512]{0,1:T(8,128)(2,1)S(1)} all-gather(bf16[49,32]{0,1:T(8,128)(2,1)} %param.9), channel_id=1, replica_groups=mesh['group'=8,'shard'=16] {'shard'}, dimensions={1}, use_global_device_ids=true | all-gather | bytes 53312 | tf_op jit(solution)/shard_map/all_gather | solution.py:189
  31.8 0.1 copy.16
  31.9 0.0 copy-start.5
  32.0 26.0 %fusion.18 = (f32[28,28]{1,0:T(8,128)S(1)}, f32[1,28,28,512]{3,0,2,1:T(1,128)S(1)}) fusion(bf16[7,7,1,512]{3,2,1,0:T(2,128)(2,1)S(1)} %reshape.159, bf16[1,28,28,512]{3,2,1,0:T(8,128)(2,1)} %param.7), kind=kOutput, calls=%fused_computation.45 | convolution fusion | flops 35069168 | bytes 2461760 | tf_op jit(solution)/shard_map/jvp()/conv_general_dilated | solution.py:16
  58.0 0.0 copy-start
  58.0 0.0 copy-start.8
  58.0 0.0 copy-done.5
  58.1 0.2 reshape.145
  58.2 11.6 %multiply_reduce_fusion.1 = f32[28,28]{1,0:T(8,128)S(1)} fusion(f32[1,28,28,512]{3,0,2,1:T(1,128)S(1)} %get-tuple-element.12, f32[28,28]{1,0:T(8,128)S(1)} %broadcast_multiply_fusion), kind=kLoop, calls=%fused_computation.26 | loop fusion | flops 1203440 | bytes 1611904 | tf_op jit(solution)/shard_map/jvp()/reduce_sum | solution.py:26
  69.9 0.1 sqrt.21
  70.0 0.0 copy-done.8
  70.0 0.0 copy-start.10
  70.0 20.9 %convert_reduce_fusion = bf16[28,28,512]{2,1,0:T(8,128)(2,1)S(1)} fusion(f32[512]{0:T(512)S(1)} %copy-done.8, f32[28,28]{1,0:T(8,128)S(1)} %get-tuple-element.10, f32[1,28,28,512]{3,0,2,1:T(1,128)S(1)} %get-tuple-element.12, f32[28,28]{1,0:T(8,128)S(1)} %broadcast_multiply_fusion), kind=kLoop, calls=%fused_computation.25 | loop fusion | flops 1605632 | bytes 2416768 | tf_op jit(solution)/shard_map/convert_element_type | solution.py:196
  90.9 0.0 copy-done
  90.9 1.0 reshape.143
  92.0 0.0 all-gather.3.cloned.1.call-done
  92.0 5.4 %multiply_convert_fusion = (bf16[784,2048]{1,0:T(8,128)(2,1)S(1)}, f32[784,2048]{1,0:T(8,128)}) fusion(bf16[784,512]{1,0:T(8,128)(2,1)} %reshape.143, bf16[512,2048]{1,0:T(8,128)(2,1)} %all-gather.3.cloned.1.call-done), kind=kOutput, calls=%fused_computation.8 | convolution fusion | flops 1652195328 | bytes 12533760 | tf_op jit(solution)/shard_map/dot_general | solution.py:197
  97.4 1.7 copy-done.12
  99.2 3.7 %multiply_convert_fusion.1 = bf16[2048,512]{1,0:T(8,128)(2,1)} fusion(bf16[784,2048]{1,0:T(8,128)(2,1)S(1)} %get-tuple-element.13, bf16[784,512]{1,0:T(8,128)(2,1)S(1)} %reshape.145), kind=kOutput, calls=%fused_computation.11 | convolution fusion | flops 1646264320 | bytes 6111232 | tf_op jit(solution)/shard_map/dot_general | solution.py:218
  102.9 6.2 %fusion.5 = bf16[784,2048]{1,0:T(8,128)(2,1)S(1)} fusion(f32[784,2048]{1,0:T(8,128)} %get-tuple-element.14, bf16[784,512]{1,0:T(8,128)(2,1)S(1)} %reshape.145, bf16[2048,512]{1,0:T(8,128)(2,1)} %all-gather.5.cloned.1.call-done), kind=kOutput, calls=%fused_computation.7 | convolution fusion | flops 1660223488 | bytes 12533760 | tf_op jit(solution)/shard_map/dot_general | solution.py:202
  109.1 1.6 copy-done.11
  110.8 3.7 %multiply_convert_fusion.2 = bf16[512,2048]{1,0:T(8,128)(2,1)} fusion(bf16[784,512]{1,0:T(8,128)(2,1)S(1)} %copy-done.7, bf16[784,2048]{1,0:T(8,128)(2,1)S(1)} %fusion.5), kind=kOutput, calls=%fused_computation.12 | convolution fusion | flops 1646264320 | bytes 6111232 | tf_op jit(solution)/shard_map/dot_general | solution.py:214
  114.5 3.3 %reshape.148 = bf16[1,512,4,512]{3,2,1,0:T(4,128)(2,1)S(1)} reshape(bf16[512,2048]{1,0:T(8,128)(2,1)} %multiply_convert_fusion.2) | data formatting | bytes 4194304 | tf_op jit(solution)/shard_map/reshape | solution.py:41
  117.8 0.0 copy-start.9
  117.8 0.4 copy.34
  118.2 1.2 copy-done.9
  119.4 5.1 %fusion.10 = (f32[784]{0:T(1024)S(1)}, f32[784,512]{1,0:T(8,128)}) fusion(f32[784]{0:T(1024)S(1)} %sqrt.21, f32[512]{0:T(512)S(1)} %copy-done.8, bf16[784,2048]{1,0:T(8,128)(2,1)} %copy-done.11, bf16[512,2048]{1,0:T(8,128)(2,1)S(1)} %copy-done.9), kind=kOutput, calls=%fused_computation.27 | convolution fusion | flops 1645370624 | bytes 6922368 | tf_op jit(solution)/shard_map/dot_general | solution.py:206
  124.5 2.3 pad_maximum_fusion
  126.9 4.9 %gather_fusion = bf16[8,512,512]{2,1,0:T(8,128)(2,1)} fusion(bf16[8,512,512]{2,1,0:T(8,128)(2,1)} %pad_maximum_fusion, s32[1024]{0:T(1024)S(1)} %pad_clamp_fusion), kind=kCustom, calls=%fused_computation | custom fusion | bytes 8388640 | tf_op jit(solution)/shard_map/jit(_take)/gather | solution.py:226
  131.8 2.7 broadcast_select_fusion.p_ref
  134.4 58.7 %shard_map.94 = f32[2,512,512]{2,1,0:T(8,128)S(1)} custom-call(bf16[8,512,512]{2,1,0:T(8,128)(2,1)S(1)} %broadcast_select_fusion.p_ref), custom_call_target="tpu_custom_call" | custom-call | tf_op jit(solution)/shard_map/pallas_call | solution.py:162
  193.1 0.1 neg.16
  193.2 5.6 %fusion.19 = f32[784,512]{1,0:T(8,128)} fusion(bf16[784,2048]{1,0:T(8,128)(2,1)} %copy-done.12, bf16[2048,512]{1,0:T(8,128)(2,1)} %all-gather.5.cloned.1.call-done), kind=kOutput, calls=%fused_computation.46 | convolution fusion | flops 1644167168 | bytes 6914048 | tf_op jit(solution)/shard_map/dot_general | solution.py:199
  198.8 2.6 reshape.144
  201.5 2.7 %add_convert_fusion = bf16[1,28,28,512]{3,2,1,0:T(8,128)(2,1)} fusion(f32[1,28,28,512]{3,2,1,0:T(8,128)} %reshape.144, bf16[1,28,28,512]{3,2,1,0:T(8,128)(2,1)S(1)} %copy-done.4), kind=kLoop, calls=%fused_computation.17 | loop fusion | flops 1204224 | bytes 3211264 | tf_op jit(solution)/shard_map/convert_element_type | solution.py:200
  204.2 4.0 %reshape.146 = f32[1,28,28,512]{3,0,2,1:T(1,128)} reshape(f32[784,512]{1,0:T(8,128)} %get-tuple-element.16) | data formatting | bytes 3211264 | tf_op jit(solution)/shard_map/reshape | solution.py:209
  208.2 13.6 %multiply_reduce_fusion = f32[28,28]{1,0:T(8,128)S(1)} fusion(f32[1,28,28,512]{3,0,2,1:T(1,128)} %reshape.146, f32[28,28]{1,0:T(8,128)S(1)} %get-tuple-element.9, f32[512]{0:T(512)S(1)} %copy-done.8, f32[1,28,28,512]{3,0,2,1:T(1,128)} %copy-done, f32[28,28]{1,0:T(8,128)S(1)} %broadcast_multiply_fusion), kind=kLoop, calls=%fused_computation.24 | loop fusion | flops 2006256 | bytes 3222720 | tf_op jit(solution)/shard_map/transpose(jvp())/reduce_sum | solution.py:27
  221.9 12.2 %multiply_reduce_fusion.2 = f32[28,28]{1,0:T(8,128)S(1)} fusion(f32[28,28]{1,0:T(8,128)S(1)} %multiply_multiply_fusion.1, f32[1,28,28,512]{3,0,2,1:T(1,128)S(1)} %copy-done.1, f32[28,28]{1,0:T(8,128)S(1)} %broadcast_multiply_fusion), kind=kLoop, calls=%fused_computation.28 | loop fusion | flops 1203440 | bytes 1615040 | tf_op jit(solution)/shard_map/transpose(jvp())/reduce_sum | solution.py:26
  234.1 0.0 copy-start.6
  234.1 4.1 %fusion.37 = f32[1,28,28,512]{3,0,2,1:T(1,128)S(1)} fusion(f32[1,28,28,512]{3,0,2,1:T(1,128)S(1)} %copy-done.2, f32[28,28]{1,0:T(8,128)S(1)} %add_multiply_fusion.1, f32[28,28]{1,0:T(8,128)S(1)} %multiply_multiply_fusion.1, f32[512]{0:T(512)S(1)} %copy-done.8, f32[28,28]{1,0:T(8,128)S(1)} %get-tuple-element.10, f32[1,28,28,512]{3,0,2,1:T(1,128)S(1)} %copy-done.1, ...), kind=kLoop, calls=%fused_computation.22.clone.1 | loop fusion | flops 2408448 | bytes 4831488 | tf_op jit(solution)/shard_map/transpose(jvp())/conv_general_dilated | solution.py:16
  238.2 0.0 copy-done.6
  238.2 22.5 %fusion.6 = bf16[1,28,28,512]{3,0,2,1:T(2,128)(2,1)S(1)} fusion(bf16[7,7,512,1]{2,3,1,0:T(2,128)(2,1)S(1)} %reshape.160, bf16[1,28,28,512]{3,2,1,0:T(8,128)(2,1)S(1)} %copy-done.6, f32[1,28,28,512]{3,0,2,1:T(1,128)S(1)} %fusion.37), kind=kOutput, calls=%fused_computation.15 | convolution fusion | flops 209215488 | bytes 3261440 | tf_op jit(solution)/shard_map/transpose(jvp())/conv_general_dilated | solution.py:16
  260.7 1.2 copy.23
  261.9 1.3 copy.36
  (24 shorter events, 0.2 us)
Async XLA Ops:
  7.2 84.8 %all-gather.3.cloned.1.call-start = ((), (), s32[]{:S(2)}) async-start(), calls=%async_computation | async-start | bytes 2228224 | tf_op jit(solution)/shard_map/all_gather | solution.py:190
  7.9 95.0 %all-gather.5.cloned.1.call-start = ((), (), s32[]{:S(2)}) async-start(), calls=%async_computation.1 | async-start | bytes 2228224 | tf_op jit(solution)/shard_map/all_gather | solution.py:191
  31.9 26.1 %copy-start.5 = (bf16[1,28,28,512]{3,2,1,0:T(8,128)(2,1)S(1)}, bf16[1,28,28,512]{3,2,1,0:T(8,128)(2,1)}, u32[]{:S(2)}) copy-start(bf16[1,28,28,512]{3,2,1,0:T(8,128)(2,1)} %param.8) | copy-start | bytes 2408452
  58.0 32.9 %copy-start = (f32[1,28,28,512]{3,0,2,1:T(1,128)}, f32[1,28,28,512]{3,0,2,1:T(1,128)S(1)}, u32[]{:S(2)}) copy-start(f32[1,28,28,512]{3,0,2,1:T(1,128)S(1)} %get-tuple-element.12) | copy-start | bytes 4816900
  58.0 12.0 %copy-start.8 = (f32[512]{0:T(512)S(1)}, f32[512]{0:T(512)}, u32[]{:S(2)}) copy-start(f32[512]{0:T(512)} %param.10) | copy-start | bytes 6148
  70.0 22.0 %copy-start.10 = (s32[8]{0:T(128)S(1)}, s32[8]{0:T(128)}, u32[]{:S(2)}) copy-start(s32[8]{0:T(128)} %param.13) | copy-start | bytes 100
  97.4 1.7 copy-start.12
  102.9 7.8 %copy-start.7 = (bf16[784,512]{1,0:T(8,128)(2,1)S(1)}, bf16[784,512]{1,0:T(8,128)(2,1)}, u32[]{:S(2)}) copy-start(bf16[784,512]{1,0:T(8,128)(2,1)} %reshape.143) | copy-start | bytes 2408452
  109.1 1.6 copy-start.11
  117.8 1.6 copy-start.9
  119.4 5.1 %copy-start.3 = (bf16[2048,512]{1,0:T(8,128)(2,1)S(1)}, bf16[2048,512]{1,0:T(8,128)(2,1)}, u32[]{:S(2)}) copy-start(bf16[2048,512]{1,0:T(8,128)(2,1)} %multiply_convert_fusion.1) | copy-start | bytes 6291460
  198.8 2.6 copy-start.4
  208.2 13.7 %copy-start.1 = (f32[1,28,28,512]{3,0,2,1:T(1,128)S(1)}, f32[1,28,28,512]{3,0,2,1:T(1,128)}, u32[]{:S(2)}) copy-start(f32[1,28,28,512]{3,0,2,1:T(1,128)} %copy-done) | copy-start | bytes 4816900
  208.2 25.9 %copy-start.2 = (f32[1,28,28,512]{3,0,2,1:T(1,128)S(1)}, f32[1,28,28,512]{3,0,2,1:T(1,128)}, u32[]{:S(2)}) copy-start(f32[1,28,28,512]{3,0,2,1:T(1,128)} %reshape.146) | copy-start | bytes 4816900
  234.1 4.1 %copy-start.6 = (bf16[1,28,28,512]{3,2,1,0:T(8,128)(2,1)S(1)}, bf16[1,28,28,512]{3,2,1,0:T(8,128)(2,1)}, u32[]{:S(2)}) copy-start(bf16[1,28,28,512]{3,2,1,0:T(8,128)(2,1)} %param.8) | copy-start | bytes 2408452
Sparse Core Ops, SparseCore 0:
  9.7 37.7 all-gather.2
  49.2 34.2 all-gather.4

commit v2 on v0

v2 whole, which is shorter than its diff:
```python
import functools

import jax
import jax.numpy as jnp
from jax import lax
from jax.experimental import pallas as pl
from jax.experimental.pallas import tpu as pltpu
from jax.sharding import PartitionSpec as P

BLK = 512
F32, BF16 = jnp.float32, jnp.bfloat16
ROWS, COLS, HALO = 28, 28, 3
PIX = ROWS * COLS
HROWS = ROWS // 2
XROWS, XCOLS = HROWS + 2 * HALO, COLS + 2 * HALO
NT = (((1,), (1,)), ((), ()))
TN = (((0,), (0,)), ((), ()))


def at8(start, size):
    return pl.ds(pl.multiple_of(start, 8), size)


def put_row(x2, half, row, line):
    for blk in range(4):
        start = (row * XCOLS + HALO) * 8 + half * 4 + blk
        x2[pl.ds(start, COLS, stride=8), :] = line[:, 128 * blk : 128 * blk + 128]


def fill_images(x2, img):
    x2[...] = jnp.zeros_like(x2)

    @pl.loop(0, HROWS + HALO)
    def _(i):
        put_row(x2, 0, i + HALO, img[i].astype(F32))
        put_row(x2, 1, i, img[i + HROWS - HALO].astype(F32))


def conv_row(x2, w2, c2, h, flip):
    for w0 in range(0, COLS, 14):
        acc = jnp.zeros((14, 8, 128), F32)
        for a in range(7):
            row = x2[at8(((h + a) * XCOLS + w0) * 8, 160), :].reshape(20, 8, 128)
            for b in range(7):
                tap = 48 - 7 * a - b if flip else 7 * a + b
                acc = acc + row[b : b + 14] * w2[8 * tap : 8 * tap + 8, :][None]
        c2[at8((h * COLS + w0) * 8, 112), :] = acc.reshape(112, 128)


def norm_rows(c2, xhat, rstd):
    @pl.loop(0, 7)
    def _(k):
        for half in range(2):
            parts = [c2[pl.ds(k * 448 + half * 4 + blk, 56, stride=8), :] for blk in range(4)]
            mean = jnp.sum(parts[0] + parts[1] + parts[2] + parts[3], axis=1, keepdims=True) * (1.0 / 512)
            parts = [v - mean for v in parts]
            sq = [v * v for v in parts]
            var = jnp.sum(sq[0] + sq[1] + sq[2] + sq[3], axis=1, keepdims=True) * (1.0 / 512)
            inv = 1.0 / jnp.sqrt(var + 1e-06)
            rows = at8(half * 392 + k * 56, 56)
            for blk in range(4):
                xhat[rows, 128 * blk : 128 * blk + 128] = parts[blk] * inv
            rstd[rows, :] = jnp.broadcast_to(inv, (56, 128))


def scale_rows(xhat, gain, lhs):
    @pl.loop(0, 7)
    def _(k):
        rows = pl.ds(pl.multiple_of(k * 112, 16), 112)
        lhs[0, rows, :] = (xhat[rows, :] * gain[...]).astype(BF16)


def flat_rows(cot, rhs):
    @pl.loop(0, 7)
    def _(k):
        lines = [cot[4 * k + r].astype(F32) for r in range(4)]
        rhs[4, pl.ds(pl.multiple_of(k * 112, 16), 112), :] = jnp.concatenate(lines, axis=0).astype(BF16)


def gelu_pair(v):
    cdf = 0.5 * (1.0 + lax.erf(v * 0.7071067811865476))
    pdf = 0.3989422804014327 * jnp.exp(-0.5 * v * v)
    return v * cdf, cdf + v * pdf


def up_step(lhs, up, slope, j):
    cols = pl.ds(pl.multiple_of(j * 256, 256), 256)
    part = pl.ds(pl.multiple_of(lax.rem(j, 2) * 256, 256), 256)
    pre = jnp.dot(lhs[0], up[:, cols], preferred_element_type=F32)
    act, der = gelu_pair(pre)
    lhs[1 + lax.div(j, 2), :, part] = act.astype(BF16)
    slope[j] = der


def back_step(rhs, down, slope, j):
    rows = pl.ds(pl.multiple_of(j * 256, 256), 256)
    part = pl.ds(pl.multiple_of(lax.rem(j, 2) * 256, 256), 256)
    back = lax.dot_general(rhs[4], down[rows, :], NT, preferred_element_type=F32)
    rhs[lax.div(j, 2), :, part] = (back * slope[j]).astype(BF16)


def grad_tile(lhs, rhs, k, scale):
    left = jnp.maximum(k - 3, 0)
    right = jnp.minimum(k, 4)
    return lax.dot_general(lhs[left], rhs[right], TN, preferred_element_type=F32) * scale


def branch_cols(lhs, down, out, j):
    cols = pl.ds(pl.multiple_of(j * 256, 256), 256)
    acc = jnp.dot(lhs[1], down[0:512, cols], preferred_element_type=F32)
    for k in range(1, 4):
        acc = acc + jnp.dot(lhs[1 + k], down[512 * k : 512 * k + 512, cols], preferred_element_type=F32)
    out[:, cols] = acc


def back_u_cols(rhs, up, out, j):
    rows = pl.ds(pl.multiple_of(j * 256, 256), 256)
    acc = lax.dot_general(rhs[0], up[rows, 0:512], NT, preferred_element_type=F32)
    for k in range(1, 4):
        acc = acc + lax.dot_general(rhs[k], up[rows, 512 * k : 512 * k + 512], NT, preferred_element_type=F32)
    out[:, rows] = acc


def mix_rows(img, branch, mixed):
    @pl.loop(0, 14)
    def _(k):
        lines = branch[at8(k * 56, 56), :]
        for r in range(2):
            mixed[2 * k + r] = (img[2 * k + r].astype(F32) + lines[28 * r : 28 * r + 28]).astype(BF16)


def norm_back_rows(back, xhat, rstd, gain):
    @pl.loop(0, 14)
    def _(k):
        rows = at8(k * 56, 56)
        grad = back[rows, :] * gain[...]
        unit = xhat[rows, :]
        first = jnp.sum(grad, axis=1, keepdims=True) * (1.0 / 512)
        second = jnp.sum(grad * unit, axis=1, keepdims=True) * (1.0 / 512)
        back[rows, :] = rstd[rows, 0:1] * (grad - first - unit * second)


def fill_back(x2, back):
    @pl.loop(0, 8)
    def _(i):
        lines = back[at8(i * 56, 56), :]
        for r in range(2):
            put_row(x2, 0, 2 * i + r + HALO, lines[28 * r : 28 * r + 28])
        lines = back[at8((i + 6) * 56, 56), :]
        for r in range(2):
            put_row(x2, 1, 2 * i + r + 1, lines[28 * r : 28 * r + 28])

    put_row(x2, 0, 16 + HALO, back[448:476, :])
    put_row(x2, 1, 0, back[308:336, :])


def conv_back_rows(x2, w2, c2, cot, out):
    @pl.loop(0, HROWS)
    def _(h):
        conv_row(x2, w2, c2, h, True)
        for half in range(2):
            line = [c2[pl.ds(h * COLS * 8 + half * 4 + blk, COLS, stride=8), :] for blk in range(4)]
            back = jnp.concatenate(line, axis=1)
            out[half * HROWS + h] = (cot[half * HROWS + h].astype(F32) + back).astype(BF16)


MESH = pl.DeviceIdType.MESH


def block_kernel(
    n, img, cot, dw, gain, up_in, down_in, owner,
    mixed, out, stat_out,
    x2, w2, c2, xhat, rstd, lhs, rhs, up, down, slope, wide, dwb, p, a0, q, a1, gfull, m, c1, ag,
    dws, dwr, ups, upr, downs, downr, a0s, a0r, a1s, a1r, gs, gr, cs, cr, ds, dr, es, er,
):
    g, s = lax.axis_index("group"), lax.axis_index("shard")
    core, pair = lax.rem(s, 2), lax.div(s, 2)
    sib = s + 1 - 2 * core
    tile = BLK
    half, chunk = tile // 2, tile // n

    def dma(src, dst, ssem, rsem, group, shard):
        return pltpu.make_async_remote_copy(
            src_ref=src, dst_ref=dst, send_sem=ssem, recv_sem=rsem, device_id=(group, shard), device_id_type=MESH
        )

    def peer(i):
        return 2 * lax.rem(pair + i, n) + core

    def gather(mine, place, send, recv):
        def out_copy(i):
            return dma(mine, place(s), send.at[0, i], recv.at[0, i], g, peer(i))

        def on_copy(i):
            j = peer(n - i)
            return dma(mine if i == 0 else place(j), place(s if i == 0 else j), send.at[1, i], recv.at[1, i], g, sib)

        def start():
            on_copy(0).start()
            for i in range(1, n):
                out_copy(i).start()

        def forward():
            for i in range(1, n):
                out_copy(i).wait_recv()
                on_copy(i).start()

        def arrived():
            for i in range(n):
                on_copy(i).wait_recv()

        def finish():
            on_copy(0).wait_send()
            for i in range(1, n):
                out_copy(i).wait_send()
                on_copy(i).wait_send()

        return start, forward, arrived, finish

    target = (pair, 2 * lax.rem(g + 1, n) + core)
    source = (lax.rem(pair + n - 1, n), 2 * g + core)
    barrier = pltpu.get_barrier_semaphore()

    def greet(group, shard):
        pl.semaphore_signal(barrier, inc=1, device_id=(group, shard), device_id_type=MESH)

    for i in range(1, 2 * n):
        greet(g, lax.rem(s + i, 2 * n))
    for i in range(1, n):
        greet(lax.rem(g + i, n), s)
    greet(*target)
    greet(*source)

    taps = dw[...].astype(F32)
    taps = jnp.concatenate([taps, taps, taps, taps], axis=1)
    lane = lax.broadcasted_iota(jnp.int32, taps.shape, 1)
    low = 32 * lax.rem(s, 4)
    taps = jnp.where((lane >= low) & (lane < low + 32), taps, 0.0)
    dwb[s] = jnp.zeros((64, 128), BF16)
    dwb[s, 0:49, :] = taps.astype(BF16)
    up[pl.ds(pl.multiple_of(s * 32, 32), 32), :] = up_in[...]
    down[pl.ds(pl.multiple_of(s * 128, 128), 128), :] = down_in[...]
    fill_images(x2, img)

    up_start, up_forward, up_arrived, up_finish = gather(
        up_in, lambda j: up.at[pl.ds(pl.multiple_of(j * 32, 32), 32)], ups, upr
    )
    down_start, down_forward, down_arrived, down_finish = gather(
        down_in, lambda j: down.at[pl.ds(pl.multiple_of(j * 128, 128), 128)], downs, downr
    )
    ag_start, ag_forward, ag_arrived, ag_finish = gather(ag.at[s], lambda j: ag.at[j], es, er)

    def dw_copy(i):
        return dma(dwb.at[s], dwb.at[s], dws.at[i], dwr.at[i], g, lax.rem(s + i, 2 * n))

    pl.semaphore_wait(barrier, 3 * n)
    for i in range(1, 2 * n):
        dw_copy(i).start()
    up_start()
    flat_rows(cot, rhs)
    for i in range(1, 2 * n):
        dw_copy(i).wait_recv()
    for blk in range(4):
        lines = [dwb[4 * blk + t].astype(F32) for t in range(4)]
        line = lines[0] + lines[1] + lines[2] + lines[3]
        w2[pl.ds(blk, 64, stride=8), :] = line
        w2[pl.ds(blk + 4, 64, stride=8), :] = line

    @pl.loop(0, 7)
    def _(h):
        conv_row(x2, w2, c2, h, False)

    down_start()

    @pl.loop(7, HROWS)
    def _(h):
        conv_row(x2, w2, c2, h, False)

    norm_rows(c2, xhat, rstd)
    scale_rows(xhat, gain, lhs)
    up_forward()
    up_arrived()

    @pl.loop(0, 8)
    def _(j):
        up_step(lhs, up, slope, j)

    down_forward()
    down_arrived()

    @pl.loop(0, 8)
    def _(j):
        back_step(rhs, down, slope, j)

    own = pl.ds(pl.multiple_of(core * half, half), half)
    other = pl.ds(pl.multiple_of((1 - core) * half, half), half)
    scale = (2 * n * PIX) ** -0.5

    def slot(i):
        return lax.rem(pair + 1 + i, n)

    def a0_copy(i):
        return dma(p.at[i, other], a0.at[i], a0s.at[i], a0r.at[i], g, sib)

    def a1_copy(i):
        return dma(q.at[i], a1.at[i], a1s.at[i], a1r.at[i], g, 2 * slot(i) + core)

    def pass_on(i):
        a0_copy(i).wait_recv()
        q[i] = (p[i, own].astype(F32) + a0[i].astype(F32)).astype(BF16)
        a1_copy(i).start()

    @pl.loop(0, n)
    def _(i):
        p[i] = grad_tile(lhs, rhs, owner[slot(i)], scale).astype(BF16)
        a0_copy(i).start()

        @pl.when(i > 0)
        def _():
            pass_on(i - 1)

    @pl.loop(0, 2)
    def _(j):
        branch_cols(lhs, down, wide, j)

    mix_rows(img, wide, mixed)

    @pl.loop(0, 2)
    def _(j):
        back_u_cols(rhs, up, wide, j)

    norm_back_rows(wide, xhat, rstd, gain)
    fill_back(x2, wide)
    conv_back_rows(x2, w2, c2, cot, out)

    a0_copy(n - 1).wait_recv()
    acc = p[n - 1, own].astype(F32) + a0[n - 1].astype(F32)
    for i in range(n - 1):
        a1_copy(i).wait_recv()
        acc = acc + a1[i].astype(F32)
    gfull[own] = acc.astype(BF16)
    g_copy = dma(gfull.at[own], gfull.at[own], gs, gr, g, sib)
    g_copy.start()
    g_copy.wait_recv()
    whole = gfull[...]
    side = jnp.where(core == 0, whole, whole.T)
    stat = lax.dot_general(side, side, NT, preferred_element_type=F32)
    m[...] = (stat * (1.0 / tile)).astype(BF16).reshape(n, chunk, tile)

    def c_copy(i):
        j = lax.rem(g + i, n)
        return dma(m.at[j], c1.at[i], cs.at[i], cr.at[i], j, s)

    for i in range(1, n):
        c_copy(i).start()
    acc = m[g].astype(F32)
    for i in range(1, n):
        c_copy(i).wait_recv()
        acc = acc + c1[i].astype(F32)
    c1[0] = acc.astype(BF16)
    d_copy = dma(c1.at[0], ag.at[target[1]], ds, dr, *target)
    d_copy.start()
    d_copy.wait_recv()
    ag_start()
    ag_forward()
    ag_arrived()
    for k in range(2 * n):
        stat_out[k % 2, pl.ds((k // 2 + n - 1) % n * chunk, chunk)] = ag[k].astype(F32)

    up_finish()
    down_finish()
    ag_finish()
    for i in range(1, 2 * n):
        dw_copy(i).wait_send()
    for i in range(n):
        a0_copy(i).wait_send()
    for i in range(n - 1):
        a1_copy(i).wait_send()
        c_copy(i + 1).wait_send()
    g_copy.wait_send()
    d_copy.wait_send()


def local(images, cotangent, dw_kernel, norm_gain, w_up, w_down, owner_table):
    n = lax.axis_size("group")
    half, chunk = BLK // 2, BLK // n
    sem = pltpu.SemaphoreType.DMA
    vmem = pltpu.VMEM
    width = images.shape[-1]
    mixed, back, stat = pl.pallas_call(
        functools.partial(block_kernel, n),
        out_shape=(
            jax.ShapeDtypeStruct((ROWS, COLS, width), BF16),
            jax.ShapeDtypeStruct((ROWS, COLS, width), BF16),
            jax.ShapeDtypeStruct((2, BLK, BLK), F32),
        ),
        in_specs=[pl.BlockSpec(memory_space=vmem)] * 6 + [pl.BlockSpec(memory_space=pltpu.SMEM)],
        out_specs=[pl.BlockSpec(memory_space=vmem)] * 3,
        scratch_shapes=[
            vmem((XROWS * XCOLS * 8, 128), F32),
            vmem((512, 128), F32),
            vmem((HROWS * COLS * 8, 128), F32),
            vmem((PIX, width), F32),
            vmem((PIX, 128), F32),
            vmem((5, PIX, width), BF16),
            vmem((5, PIX, width), BF16),
            vmem((512, 2048), BF16),
            vmem((2048, 512), BF16),
            vmem((8, PIX, 256), F32),
            vmem((PIX, width), F32),
            vmem((2 * n, 64, 128), BF16),
            vmem((n, BLK, BLK), BF16),
            vmem((n, half, BLK), BF16),
            vmem((n - 1, half, BLK), BF16),
            vmem((n - 1, half, BLK), BF16),
            vmem((BLK, BLK), BF16),
            vmem((n, chunk, BLK), BF16),
            vmem((n, chunk, BLK), BF16),
            vmem((2 * n, chunk, BLK), BF16),
            sem((2 * n,)), sem((2 * n,)),
            sem((2, n)), sem((2, n)),
            sem((2, n)), sem((2, n)),
            sem((n,)), sem((n,)),
            sem((n - 1,)), sem((n - 1,)),
            sem, sem,
            sem((n,)), sem((n,)),
            sem, sem,
            sem((2, n)), sem((2, n)),
        ],
        compiler_params=pltpu.CompilerParams(collective_id=0, has_side_effects=True, vmem_limit_bytes=60 * 2**20),
    )(images[0], cotangent[0], dw_kernel, norm_gain.reshape(1, width), w_up, w_down, owner_table)
    return (mixed[None], back[None], stat[None])


def solution(mesh):
    return jax.shard_map(
        local,
        mesh=mesh,
        in_specs=(
            P(("group", "shard"), None, None, None),
            P(("group", "shard"), None, None, None),
            P(None, "shard"),
            P(),
            P("shard", None),
            P("shard", None),
            P(),
        ),
        out_specs=(
            P(("group", "shard"), None, None, None),
            P(("group", "shard"), None, None, None),
            P("group", None, None, None),
        ),
        check_vma=False,
    )
```

time: 680 us -> 111 us (0.16)
  the two profiles are of different devices: /device:TPU:5 before, /device:TPU:1 now
where the time goes in v2:
time: 111 us; the launch traced here: 110 us
  Pallas kernels  102 us (92%)
  local copies, waits for them, and re-layouts  7.26 us (7%)
    pallas_call x1, Pallas kernels, local(): pl.pallas_call(functools.partial(block_kernel, n), out_shape=(jax.ShapeDt...  102 us
    unnamed x6, local copies, waits for them, and re-layouts  7.26 us

profile of v2, /device:TPU:1, one launch (start us, length us, event | category | flops | bytes accessed | tf_op | source)
XLA Modules:
  0.0 110.1 jit_solution(5140376764693263816)
XLA Ops:
  0.6 1.4 %copy.10.dw = bf16[49,32]{1,0:T(8,128)(2,1)} copy(bf16[49,32]{0,1:T(8,128)(2,1)} %param.9) | data formatting | bytes 6272 | tf_op args[2]
  2.0 102.1 %shard_map.94 = (bf16[28,28,512]{2,1,0:T(8,128)(2,1)}, bf16[28,28,512]{2,1,0:T(8,128)(2,1)}, f32[2,512,512]{2,1,0:T(8,128)}) custom-call(bf16[28,28,512]{2,1,0:T(8,128)(2,1)} %bitcast.7, bf16[28,28,512]{2,1,0:T(8,128)(2,1)} %bitcast.8, bf16[49,32]{1,0:T(8,128)(2,1)} %copy.10.dw, f32[1,512]{1,0:T(1,128)} %bitcast.11, bf16[32,2048]{1,0:T(8,128)(2,1)} %up_in.1, ...), custom_call_target="tpu_custom_call" | custom-call | tf_op jit(solution)/shard_map/pallas_call | solution.py:390
  104.2 0.0 copy-start
  104.2 2.3 %copy.14 = bf16[1,28,28,512]{3,2,1,0:T(8,128)(2,1)} copy(bf16[1,28,28,512]{3,2,1,0:T(8,128)(2,1)} %bitcast.10) | data formatting | bytes 1605632
  106.5 2.2 %copy.15 = bf16[1,28,28,512]{3,2,1,0:T(8,128)(2,1)} copy(bf16[1,28,28,512]{3,2,1,0:T(8,128)(2,1)} %bitcast.9) | data formatting | bytes 1605632
  108.7 0.0 copy-done
  108.7 1.3 %copy.16 = f32[1,2,512,512]{3,2,1,0:T(8,128)} copy(f32[1,2,512,512]{3,2,1,0:T(8,128)S(1)} %bitcast.6) | data formatting | bytes 4194304
Async XLA Ops:
  104.2 4.6 %copy-start = (f32[2,512,512]{2,1,0:T(8,128)S(1)}, f32[2,512,512]{2,1,0:T(8,128)}, u32[]{:S(2)}) copy-start(f32[2,512,512]{2,1,0:T(8,128)} %get-tuple-element.8) | copy-start | bytes 6291460

commit v3 on v2

--- a/solution.py
+++ b/solution.py
@@ -165,19 +165,53 @@
 
 
 MESH = pl.DeviceIdType.MESH
+PAIRS = [(i, j) for i in range(BLK // 128) for j in range(i, BLK // 128)]
+
+
+def finish_kernel(mixed_in, out_in, packed_in, mixed, out, stat, lines, packed, blocks, into, back):
+    load = pltpu.make_async_copy(packed_in, packed, into.at[8])
+    load.start()
+    loads, stores = [], []
+    for k in range(8):
+        rows = pl.ds(7 * (k % 4), 7)
+        src, dst = (mixed_in, mixed) if k < 4 else (out_in, out)
+        loads.append(pltpu.make_async_copy(src.at[rows], lines.at[k], into.at[k]))
+        stores.append(pltpu.make_async_copy(lines.at[k], dst.at[rows], back.at[k]))
+    for copy in loads:
+        copy.start()
+    load.wait()
+    for side in range(2):
+        for b, (i, j) in enumerate(PAIRS):
+            part = packed[side, 128 * b : 128 * b + 128, :].astype(F32)
+            blocks[side, 128 * i : 128 * i + 128, 128 * j : 128 * j + 128] = part
+            if i != j:
+                blocks[side, 128 * j : 128 * j + 128, 128 * i : 128 * i + 128] = part.T
+        stores.append(pltpu.make_async_copy(blocks.at[side], stat.at[side], back.at[8 + side]))
+        stores[-1].start()
+        for k in range(4 * side, 4 * side + 4):
+            loads[k].wait()
+            stores[k].start()
+    for copy in stores:
+        copy.wait()
 
 
 def block_kernel(
-    n, img, cot, dw, gain, up_in, down_in, owner,
-    mixed, out, stat_out,
-    x2, w2, c2, xhat, rstd, lhs, rhs, up, down, slope, wide, dwb, p, a0, q, a1, gfull, m, c1, ag,
-    dws, dwr, ups, upr, downs, downr, a0s, a0r, a1s, a1r, gs, gr, cs, cr, ds, dr, es, er,
+    n, img_hbm, cot_hbm, dw, gain, up_in, down_in, owner,
+    mixed_hbm, out_hbm, ag,
+    x2, w2, c2, xhat, rstd, lhs, rhs, up, down, slope, wide, dwb, p, a0, q, a1, gfull, m, c1, img, cot, mixed, out,
+    dws, dwr, ups, upr, downs, downr, a0s, a0r, a1s, a1r, gs, gr, cs, cr, ds, dr, es, er, ios,
 ):
+    img_copy = pltpu.make_async_copy(img_hbm, img, ios.at[0])
+    cot_copy = pltpu.make_async_copy(cot_hbm, cot, ios.at[1])
+    mixed_copy = pltpu.make_async_copy(mixed, mixed_hbm, ios.at[2])
+    out_copy = pltpu.make_async_copy(out, out_hbm, ios.at[3])
+    img_copy.start()
+    cot_copy.start()
     g, s = lax.axis_index("group"), lax.axis_index("shard")
     core, pair = lax.rem(s, 2), lax.div(s, 2)
     sib = s + 1 - 2 * core
     tile = BLK
-    half, chunk = tile // 2, tile // n
+    half, chunk = tile // 2, len(PAIRS) * 128 // n
 
     def dma(src, dst, ssem, rsem, group, shard):
         return pltpu.make_async_remote_copy(
@@ -216,6 +250,64 @@
                 on_copy(i).wait_send()
 
         return start, forward, arrived, finish
+
+    zpos, ypos = lax.div(pair, 2), lax.rem(pair, 2)
+    across = s + 2 - 4 * ypos
+    beyond = g + 1 - 2 * lax.rem(g, 2)
+
+    def spread(place, send, recv):
+        def block(i, y):
+            return 4 * lax.rem(zpos + 4 - i, 4) + 2 * y + core
+
+        def z_copy(i):
+            return dma(place(s), place(s), send.at[0, i], recv.at[0, i], g, 4 * lax.rem(zpos + i, 4) + 2 * ypos + core)
+
+        def y_copy(i, h):
+            ref = place(block(i, ypos), h)
+            return dma(ref, ref, send.at[1 + h, i], recv.at[1 + h, i], beyond if h else g, across)
+
+        def core_z(i):
+            ref = place(block(i, ypos))
+            return dma(ref, ref, send.at[3, i], recv.at[3, i], g, sib)
+
+        def core_y(i, h):
+            ref = place(block(i, 1 - ypos), h)
+            return dma(ref, ref, send.at[4 + h, i], recv.at[4 + h, i], g, sib)
+
+        def start():
+            for i in range(1, 4):
+                z_copy(i).start()
+            y_copy(0, 0).start()
+            y_copy(0, 1).start()
+            core_z(0).start()
+
+        def relay_z(i):
+            z_copy(i).wait_recv()
+            y_copy(i, 0).start()
+            y_copy(i, 1).start()
+            core_z(i).start()
+
+        def relay_y(i):
+            for h in range(2):
+                y_copy(i, h).wait_recv()
+                core_y(i, h).start()
+
+        def arrived():
+            for i in range(4):
+                core_z(i).wait_recv()
+                core_y(i, 0).wait_recv()
+                core_y(i, 1).wait_recv()
+
+        def finish():
+            for i in range(4):
+                if i:
+                    z_copy(i).wait_send()
+                core_z(i).wait_send()
+                for h in range(2):
+                    y_copy(i, h).wait_send()
+                    core_y(i, h).wait_send()
+
+        return start, relay_z, relay_y, arrived, finish
 
     target = (pair, 2 * lax.rem(g + 1, n) + core)
     source = (lax.rem(pair + n - 1, n), 2 * g + core)
@@ -230,8 +322,9 @@
         greet(lax.rem(g + i, n), s)
     greet(*target)
     greet(*source)
-
-    taps = dw[...].astype(F32)
+    greet(beyond, across)
+
+    taps = dw[...].astype(F32).T
     taps = jnp.concatenate([taps, taps, taps, taps], axis=1)
     lane = lax.broadcasted_iota(jnp.int32, taps.shape, 1)
     low = 32 * lax.rem(s, 4)
@@ -240,23 +333,32 @@
     dwb[s, 0:49, :] = taps.astype(BF16)
     up[pl.ds(pl.multiple_of(s * 32, 32), 32), :] = up_in[...]
     down[pl.ds(pl.multiple_of(s * 128, 128), 128), :] = down_in[...]
+    img_copy.wait()
     fill_images(x2, img)
 
-    up_start, up_forward, up_arrived, up_finish = gather(
-        up_in, lambda j: up.at[pl.ds(pl.multiple_of(j * 32, 32), 32)], ups, upr
-    )
-    down_start, down_forward, down_arrived, down_finish = gather(
-        down_in, lambda j: down.at[pl.ds(pl.multiple_of(j * 128, 128), 128)], downs, downr
-    )
-    ag_start, ag_forward, ag_arrived, ag_finish = gather(ag.at[s], lambda j: ag.at[j], es, er)
+    def up_place(j, h=None):
+        return up.at[pl.ds(pl.multiple_of(j * 32 + (h or 0) * 16, 16), 32 if h is None else 16)]
+
+    def down_place(j, h=None):
+        return down.at[pl.ds(pl.multiple_of(j * 128 + (h or 0) * 64, 64), 128 if h is None else 64)]
+
+    up_start, up_relay_z, up_relay_y, up_arrived, up_finish = spread(up_place, ups, upr)
+    down_start, down_relay_z, down_relay_y, down_arrived, down_finish = spread(down_place, downs, downr)
+
+    def ag_place(j):
+        start = lax.rem(lax.div(j, 2) + n - 1, n) * chunk
+        return ag.at[lax.rem(j, 2), pl.ds(pl.multiple_of(start, chunk), chunk)]
+
+    ag_start, ag_forward, ag_arrived, ag_finish = gather(ag_place(s), ag_place, es, er)
 
     def dw_copy(i):
         return dma(dwb.at[s], dwb.at[s], dws.at[i], dwr.at[i], g, lax.rem(s + i, 2 * n))
 
-    pl.semaphore_wait(barrier, 3 * n)
+    pl.semaphore_wait(barrier, 3 * n + 1)
     for i in range(1, 2 * n):
         dw_copy(i).start()
     up_start()
+    cot_copy.wait()
     flat_rows(cot, rhs)
     for i in range(1, 2 * n):
         dw_copy(i).wait_recv()
@@ -266,26 +368,42 @@
         w2[pl.ds(blk, 64, stride=8), :] = line
         w2[pl.ds(blk + 4, 64, stride=8), :] = line
 
-    @pl.loop(0, 7)
-    def _(h):
-        conv_row(x2, w2, c2, h, False)
-
+    def conv_rows(lo, hi):
+        @pl.loop(lo, hi)
+        def _(h):
+            conv_row(x2, w2, c2, h, False)
+
+    conv_rows(0, 5)
+    up_relay_z(1)
+    up_relay_z(3)
+    conv_rows(5, 9)
+    up_relay_z(2)
     down_start()
-
-    @pl.loop(7, HROWS)
-    def _(h):
-        conv_row(x2, w2, c2, h, False)
-
+    conv_rows(9, HROWS)
+    up_relay_y(0)
+    up_relay_y(1)
+    up_relay_y(3)
     norm_rows(c2, xhat, rstd)
     scale_rows(xhat, gain, lhs)
-    up_forward()
+    up_relay_y(2)
     up_arrived()
 
-    @pl.loop(0, 8)
-    def _(j):
-        up_step(lhs, up, slope, j)
-
-    down_forward()
+    def up_steps(lo, hi):
+        @pl.loop(lo, hi)
+        def _(j):
+            up_step(lhs, up, slope, j)
+
+    up_steps(0, 2)
+    down_relay_z(1)
+    down_relay_z(3)
+    up_steps(2, 4)
+    down_relay_z(2)
+    down_relay_y(0)
+    up_steps(4, 7)
+    down_relay_y(1)
+    down_relay_y(3)
+    up_steps(7, 8)
+    down_relay_y(2)
     down_arrived()
 
     @pl.loop(0, 8)
@@ -324,6 +442,7 @@
         branch_cols(lhs, down, wide, j)
 
     mix_rows(img, wide, mixed)
+    mixed_copy.start()
 
     @pl.loop(0, 2)
     def _(j):
@@ -332,6 +451,7 @@
     norm_back_rows(wide, xhat, rstd, gain)
     fill_back(x2, wide)
     conv_back_rows(x2, w2, c2, cot, out)
+    out_copy.start()
 
     a0_copy(n - 1).wait_recv()
     acc = p[n - 1, own].astype(F32) + a0[n - 1].astype(F32)
@@ -345,28 +465,32 @@
     whole = gfull[...]
     side = jnp.where(core == 0, whole, whole.T)
     stat = lax.dot_general(side, side, NT, preferred_element_type=F32)
-    m[...] = (stat * (1.0 / tile)).astype(BF16).reshape(n, chunk, tile)
+    stat = (stat * (1.0 / tile)).astype(BF16)
+    for b, (i, j) in enumerate(PAIRS):
+        m[128 * b : 128 * b + 128, :] = stat[128 * i : 128 * i + 128, 128 * j : 128 * j + 128]
+
+    def m_chunk(j):
+        return pl.ds(pl.multiple_of(j * chunk, chunk), chunk)
 
     def c_copy(i):
         j = lax.rem(g + i, n)
-        return dma(m.at[j], c1.at[i], cs.at[i], cr.at[i], j, s)
+        return dma(m.at[m_chunk(j)], c1.at[i], cs.at[i], cr.at[i], j, s)
 
     for i in range(1, n):
         c_copy(i).start()
-    acc = m[g].astype(F32)
+    acc = m[m_chunk(g), :].astype(F32)
     for i in range(1, n):
         c_copy(i).wait_recv()
         acc = acc + c1[i].astype(F32)
     c1[0] = acc.astype(BF16)
-    d_copy = dma(c1.at[0], ag.at[target[1]], ds, dr, *target)
+    d_copy = dma(c1.at[0], ag_place(target[1]), ds, dr, *target)
     d_copy.start()
     d_copy.wait_recv()
     ag_start()
     ag_forward()
     ag_arrived()
-    for k in range(2 * n):
-        stat_out[k % 2, pl.ds((k // 2 + n - 1) % n * chunk, chunk)] = ag[k].astype(F32)
-
+    mixed_copy.wait()
+    out_copy.wait()
     up_finish()
     down_finish()
     ag_finish()
@@ -383,19 +507,19 @@
 
 def local(images, cotangent, dw_kernel, norm_gain, w_up, w_down, owner_table):
     n = lax.axis_size("group")
-    half, chunk = BLK // 2, BLK // n
+    half, chunk = BLK // 2, len(PAIRS) * 128 // n
     sem = pltpu.SemaphoreType.DMA
     vmem = pltpu.VMEM
     width = images.shape[-1]
-    mixed, back, stat = pl.pallas_call(
+    mixed, back, packed = pl.pallas_call(
         functools.partial(block_kernel, n),
         out_shape=(
             jax.ShapeDtypeStruct((ROWS, COLS, width), BF16),
             jax.ShapeDtypeStruct((ROWS, COLS, width), BF16),
-            jax.ShapeDtypeStruct((2, BLK, BLK), F32),
+            jax.ShapeDtypeStruct((2, n * chunk, 128), BF16),
         ),
-        in_specs=[pl.BlockSpec(memory_space=vmem)] * 6 + [pl.BlockSpec(memory_space=pltpu.SMEM)],
-        out_specs=[pl.BlockSpec(memory_space=vmem)] * 3,
+        in_specs=[pl.BlockSpec(memory_space=pl.ANY)] * 2 + [pl.BlockSpec(memory_space=vmem)] * 4 + [pl.BlockSpec(memory_space=pltpu.SMEM)],
+        out_specs=[pl.BlockSpec(memory_space=pl.ANY)] * 2 + [pl.BlockSpec(memory_space=vmem)],
         scratch_shapes=[
             vmem((XROWS * XCOLS * 8, 128), F32),
             vmem((512, 128), F32),
@@ -414,21 +538,42 @@
             vmem((n - 1, half, BLK), BF16),
             vmem((n - 1, half, BLK), BF16),
             vmem((BLK, BLK), BF16),
-            vmem((n, chunk, BLK), BF16),
-            vmem((n, chunk, BLK), BF16),
-            vmem((2 * n, chunk, BLK), BF16),
+            vmem((n * chunk, 128), BF16),
+            vmem((n, chunk, 128), BF16),
+            vmem((ROWS, COLS, width), BF16),
+            vmem((ROWS, COLS, width), BF16),
+            vmem((ROWS, COLS, width), BF16),
+            vmem((ROWS, COLS, width), BF16),
             sem((2 * n,)), sem((2 * n,)),
-            sem((2, n)), sem((2, n)),
-            sem((2, n)), sem((2, n)),
+            sem((6, 4)), sem((6, 4)),
+            sem((6, 4)), sem((6, 4)),
             sem((n,)), sem((n,)),
             sem((n - 1,)), sem((n - 1,)),
             sem, sem,
             sem((n,)), sem((n,)),
             sem, sem,
             sem((2, n)), sem((2, n)),
+            sem((4,)),
         ],
         compiler_params=pltpu.CompilerParams(collective_id=0, has_side_effects=True, vmem_limit_bytes=60 * 2**20),
-    )(images[0], cotangent[0], dw_kernel, norm_gain.reshape(1, width), w_up, w_down, owner_table)
+    )(images[0], cotangent[0], dw_kernel.T, norm_gain.reshape(1, width), w_up, w_down, owner_table)
+    mixed, back, stat = pl.pallas_call(
+        finish_kernel,
+        out_shape=(
+            jax.ShapeDtypeStruct((ROWS, COLS, width), BF16),
+            jax.ShapeDtypeStruct((ROWS, COLS, width), BF16),
+            jax.ShapeDtypeStruct((2, BLK, BLK), F32),
+        ),
+        in_specs=[pl.BlockSpec(memory_space=pl.ANY)] * 3,
+        out_specs=[pl.BlockSpec(memory_space=pl.ANY)] * 3,
+        scratch_shapes=[
+            vmem((8, 7, COLS, width), BF16),
+            vmem((2, n * chunk, 128), BF16),
+            vmem((2, BLK, BLK), F32),
+            sem((9,)), sem((10,)),
+        ],
+        compiler_params=pltpu.CompilerParams(vmem_limit_bytes=60 * 2**20),
+    )(mixed, back, packed)
     return (mixed[None], back[None], stat[None])
 
 

time: 111 us -> 98 us (0.88)
  local copies, waits for them, and re-layouts: 7.26 us -> 0 us
  Pallas kernels: 102 us -> 96.7 us
    pallas_call x1, Pallas kernels: 102 us -> 93.4 us  [local(): pl.pallas_call(functools.partial(block_kernel, n), out_shape=(jax.ShapeDt...]
    unnamed x6 -> x0, local copies, waits for them, and re-layouts: 7.26 us -> none
    pallas_call x0 -> x1, Pallas kernels: none -> 3.32 us  [local(): pl.pallas_call(finish_kernel, out_shape=(jax.ShapeDtypeStruct((ROWS, COLS...]
where the time goes in v3:
time: 98 us; the launch traced here: 97.3 us
  Pallas kernels  96.7 us (99%)
    pallas_call x1, Pallas kernels, local(): pl.pallas_call(functools.partial(block_kernel, n), out_shape=(jax.ShapeDt...  93.4 us
    pallas_call x1, Pallas kernels, local(): pl.pallas_call(finish_kernel, out_shape=(jax.ShapeDtypeStruct((ROWS, COLS...  3.32 us

profile of v3, /device:TPU:1, one launch (start us, length us, event | category | flops | bytes accessed | tf_op | source)
XLA Modules:
  0.0 97.3 jit_solution(9821788966069973692)
XLA Ops:
  0.6 93.4 %shard_map.94 = (bf16[28,28,512]{2,1,0:T(8,128)(2,1)}, bf16[28,28,512]{2,1,0:T(8,128)(2,1)}, bf16[2,1280,128]{2,1,0:T(8,128)(2,1)}) custom-call(bf16[28,28,512]{2,1,0:T(8,128)(2,1)} %bitcast.7, bf16[28,28,512]{2,1,0:T(8,128)(2,1)} %bitcast.8, bf16[32,49]{1,0:T(8,128)(2,1)} %bitcast.9, f32[1,512]{1,0:T(1,128)} %bitcast.10, bf16[32,2048]{1,0:T(8,128)(2,1)} %up_in.1, ...), custom_call_target="tpu_custom_call" | custom-call | tf_op jit(solution)/shard_map/pallas_call | solution.py:514
  94.0 3.3 %shard_map.95 = (bf16[28,28,512]{2,1,0:T(8,128)(2,1)}, bf16[28,28,512]{2,1,0:T(8,128)(2,1)}, f32[2,512,512]{2,1,0:T(8,128)}) custom-call(bf16[28,28,512]{2,1,0:T(8,128)(2,1)} %get-tuple-element.9.mixed_in, bf16[28,28,512]{2,1,0:T(8,128)(2,1)} %get-tuple-element.10.out_in, bf16[2,1280,128]{2,1,0:T(8,128)(2,1)} %get-tuple-element.11.packed_in), custom_call_target="tpu_custom_call" | custom-call | tf_op jit(solution)/shard_map/pallas_call | solution.py:560

commit v4 on v3

--- a/solution.py
+++ b/solution.py
@@ -47,8 +47,8 @@
         c2[at8((h * COLS + w0) * 8, 112), :] = acc.reshape(112, 128)
 
 
-def norm_rows(c2, xhat, rstd):
-    @pl.loop(0, 7)
+def norm_rows(c2, xhat, rstd, lo, hi):
+    @pl.loop(lo, hi)
     def _(k):
         for half in range(2):
             parts = [c2[pl.ds(k * 448 + half * 4 + blk, 56, stride=8), :] for blk in range(4)]
@@ -198,7 +198,7 @@
 def block_kernel(
     n, img_hbm, cot_hbm, dw, gain, up_in, down_in, owner,
     mixed_hbm, out_hbm, ag,
-    x2, w2, c2, xhat, rstd, lhs, rhs, up, down, slope, wide, dwb, p, a0, q, a1, gfull, m, c1, img, cot, mixed, out,
+    x2, w2, c2, xhat, rstd, lhs, rhs, up, down, slope, wide, dwb, flat, p, a0, q, a1, gfull, m, c1, img, cot, mixed, out,
     dws, dwr, ups, upr, downs, downr, a0s, a0r, a1s, a1r, gs, gr, cs, cr, ds, dr, es, er, ios,
 ):
     img_copy = pltpu.make_async_copy(img_hbm, img, ios.at[0])
@@ -275,11 +275,14 @@
             return dma(ref, ref, send.at[4 + h, i], recv.at[4 + h, i], g, sib)
 
         def start():
-            for i in range(1, 4):
-                z_copy(i).start()
+            z_copy(1).start()
+            z_copy(3).start()
             y_copy(0, 0).start()
             y_copy(0, 1).start()
             core_z(0).start()
+
+        def start_far():
+            z_copy(2).start()
 
         def relay_z(i):
             z_copy(i).wait_recv()
@@ -307,10 +310,9 @@
                     y_copy(i, h).wait_send()
                     core_y(i, h).wait_send()
 
-        return start, relay_z, relay_y, arrived, finish
-
-    target = (pair, 2 * lax.rem(g + 1, n) + core)
-    source = (lax.rem(pair + n - 1, n), 2 * g + core)
+        return start, start_far, relay_z, relay_y, arrived, finish
+
+    mirror = (pair, 2 * g + core)
     barrier = pltpu.get_barrier_semaphore()
 
     def greet(group, shard):
@@ -320,17 +322,16 @@
         greet(g, lax.rem(s + i, 2 * n))
     for i in range(1, n):
         greet(lax.rem(g + i, n), s)
-    greet(*target)
-    greet(*source)
+
+    @pl.when(pair != g)
+    def _():
+        greet(*mirror)
+
     greet(beyond, across)
 
-    taps = dw[...].astype(F32).T
-    taps = jnp.concatenate([taps, taps, taps, taps], axis=1)
-    lane = lax.broadcasted_iota(jnp.int32, taps.shape, 1)
-    low = 32 * lax.rem(s, 4)
-    taps = jnp.where((lane >= low) & (lane < low + 32), taps, 0.0)
-    dwb[s] = jnp.zeros((64, 128), BF16)
-    dwb[s, 0:49, :] = taps.astype(BF16)
+    flat[...] = jnp.zeros_like(flat)
+    flat[0:49, :] = dw[...].astype(F32).T
+    dwb[s] = jnp.concatenate([flat[16 * t : 16 * t + 16, :] for t in range(4)], axis=1).astype(BF16)
     up[pl.ds(pl.multiple_of(s * 32, 32), 32), :] = up_in[...]
     down[pl.ds(pl.multiple_of(s * 128, 128), 128), :] = down_in[...]
     img_copy.wait()
@@ -342,11 +343,11 @@
     def down_place(j, h=None):
         return down.at[pl.ds(pl.multiple_of(j * 128 + (h or 0) * 64, 64), 128 if h is None else 64)]
 
-    up_start, up_relay_z, up_relay_y, up_arrived, up_finish = spread(up_place, ups, upr)
-    down_start, down_relay_z, down_relay_y, down_arrived, down_finish = spread(down_place, downs, downr)
+    up_start, up_far, up_relay_z, up_relay_y, up_arrived, up_finish = spread(up_place, ups, upr)
+    down_start, down_far, down_relay_z, down_relay_y, down_arrived, down_finish = spread(down_place, downs, downr)
 
     def ag_place(j):
-        start = lax.rem(lax.div(j, 2) + n - 1, n) * chunk
+        start = lax.div(j, 2) * chunk
         return ag.at[lax.rem(j, 2), pl.ds(pl.multiple_of(start, chunk), chunk)]
 
     ag_start, ag_forward, ag_arrived, ag_finish = gather(ag_place(s), ag_place, es, er)
@@ -354,7 +355,7 @@
     def dw_copy(i):
         return dma(dwb.at[s], dwb.at[s], dws.at[i], dwr.at[i], g, lax.rem(s + i, 2 * n))
 
-    pl.semaphore_wait(barrier, 3 * n + 1)
+    pl.semaphore_wait(barrier, 3 * n - jnp.where(pair == g, 1, 0))
     for i in range(1, 2 * n):
         dw_copy(i).start()
     up_start()
@@ -362,30 +363,42 @@
     flat_rows(cot, rhs)
     for i in range(1, 2 * n):
         dw_copy(i).wait_recv()
+    lane = lax.broadcasted_iota(jnp.int32, (16, 128), 1)
     for blk in range(4):
         lines = [dwb[4 * blk + t].astype(F32) for t in range(4)]
-        line = lines[0] + lines[1] + lines[2] + lines[3]
-        w2[pl.ds(blk, 64, stride=8), :] = line
-        w2[pl.ds(blk + 4, 64, stride=8), :] = line
+        for k in range(4):
+            line = jnp.zeros((16, 128), F32)
+            for t in range(4):
+                moved = lines[t] if t == k else pltpu.roll(lines[t], 32 * ((t - k) % 4), 1)
+                line = jnp.where((lane >= 32 * t) & (lane < 32 * t + 32), moved, line)
+            w2[pl.ds(128 * k + blk, 16, stride=8), :] = line
+            w2[pl.ds(128 * k + blk + 4, 16, stride=8), :] = line
 
     def conv_rows(lo, hi):
         @pl.loop(lo, hi)
         def _(h):
             conv_row(x2, w2, c2, h, False)
 
-    conv_rows(0, 5)
+    up_far()
+    conv_rows(0, 3)
     up_relay_z(1)
     up_relay_z(3)
-    conv_rows(5, 9)
+    conv_rows(3, 6)
+    down_start()
+    conv_rows(6, 9)
     up_relay_z(2)
-    down_start()
-    conv_rows(9, HROWS)
+    conv_rows(9, 12)
     up_relay_y(0)
     up_relay_y(1)
     up_relay_y(3)
-    norm_rows(c2, xhat, rstd)
+    down_far()
+    conv_rows(12, HROWS)
+    norm_rows(c2, xhat, rstd, 0, 4)
+    up_relay_y(2)
+    down_relay_z(1)
+    down_relay_z(3)
+    norm_rows(c2, xhat, rstd, 4, 7)
     scale_rows(xhat, gain, lhs)
-    up_relay_y(2)
     up_arrived()
 
     def up_steps(lo, hi):
@@ -394,15 +407,12 @@
             up_step(lhs, up, slope, j)
 
     up_steps(0, 2)
-    down_relay_z(1)
-    down_relay_z(3)
-    up_steps(2, 4)
     down_relay_z(2)
+    up_steps(2, 6)
     down_relay_y(0)
-    up_steps(4, 7)
     down_relay_y(1)
     down_relay_y(3)
-    up_steps(7, 8)
+    up_steps(6, 8)
     down_relay_y(2)
     down_arrived()
 
@@ -483,9 +493,17 @@
         c_copy(i).wait_recv()
         acc = acc + c1[i].astype(F32)
     c1[0] = acc.astype(BF16)
-    d_copy = dma(c1.at[0], ag_place(target[1]), ds, dr, *target)
-    d_copy.start()
-    d_copy.wait_recv()
+    d_copy = dma(c1.at[0], ag_place(mirror[1]), ds, dr, *mirror)
+
+    @pl.when(pair != g)
+    def _():
+        d_copy.start()
+        d_copy.wait_recv()
+
+    @pl.when(pair == g)
+    def _():
+        ag[core, m_chunk(g), :] = c1[0]
+
     ag_start()
     ag_forward()
     ag_arrived()
@@ -502,7 +520,10 @@
         a1_copy(i).wait_send()
         c_copy(i + 1).wait_send()
     g_copy.wait_send()
-    d_copy.wait_send()
+
+    @pl.when(pair != g)
+    def _():
+        d_copy.wait_send()
 
 
 def local(images, cotangent, dw_kernel, norm_gain, w_up, w_down, owner_table):
@@ -532,7 +553,8 @@
             vmem((2048, 512), BF16),
             vmem((8, PIX, 256), F32),
             vmem((PIX, width), F32),
-            vmem((2 * n, 64, 128), BF16),
+            vmem((2 * n, 16, 128), BF16),
+            vmem((64, 32), F32),
             vmem((n, BLK, BLK), BF16),
             vmem((n, half, BLK), BF16),
             vmem((n - 1, half, BLK), BF16),

time: 98 us -> 92.2 us (0.941)
  Pallas kernels: 96.7 us -> 91.4 us
    pallas_call x1, Pallas kernels: 93.4 us -> 88.1 us  [local(): pl.pallas_call(functools.partial(block_kernel, n), out_shape=(jax.ShapeDt...]
where the time goes in v4:
time: 92.2 us; the launch traced here: 92 us
  Pallas kernels  91.4 us (99%)
    pallas_call x1, Pallas kernels, local(): pl.pallas_call(functools.partial(block_kernel, n), out_shape=(jax.ShapeDt...  88.1 us
    pallas_call x1, Pallas kernels, local(): pl.pallas_call(finish_kernel, out_shape=(jax.ShapeDtypeStruct((ROWS, COLS...  3.32 us

profile of v4, /device:TPU:1, one launch (start us, length us, event | category | flops | bytes accessed | tf_op | source)
XLA Modules:
  0.0 92.0 jit_solution(9961282882487116523)
XLA Ops:
  0.6 88.1 %shard_map.94 = (bf16[28,28,512]{2,1,0:T(8,128)(2,1)}, bf16[28,28,512]{2,1,0:T(8,128)(2,1)}, bf16[2,1280,128]{2,1,0:T(8,128)(2,1)}) custom-call(bf16[28,28,512]{2,1,0:T(8,128)(2,1)} %bitcast.7, bf16[28,28,512]{2,1,0:T(8,128)(2,1)} %bitcast.8, bf16[32,49]{1,0:T(8,128)(2,1)} %bitcast.9, f32[1,512]{1,0:T(1,128)} %bitcast.10, bf16[32,2048]{1,0:T(8,128)(2,1)} %up_in.1, ...), custom_call_target="tpu_custom_call" | custom-call | tf_op jit(solution)/shard_map/pallas_call | solution.py:535
  88.7 3.3 %shard_map.95 = (bf16[28,28,512]{2,1,0:T(8,128)(2,1)}, bf16[28,28,512]{2,1,0:T(8,128)(2,1)}, f32[2,512,512]{2,1,0:T(8,128)}) custom-call(bf16[28,28,512]{2,1,0:T(8,128)(2,1)} %get-tuple-element.9.mixed_in, bf16[28,28,512]{2,1,0:T(8,128)(2,1)} %get-tuple-element.10.out_in, bf16[2,1280,128]{2,1,0:T(8,128)(2,1)} %get-tuple-element.11.packed_in), custom_call_target="tpu_custom_call" | custom-call | tf_op jit(solution)/shard_map/pallas_call | solution.py:582

commit v5 on v4

--- a/solution.py
+++ b/solution.py
@@ -154,8 +154,8 @@
     put_row(x2, 1, 0, back[308:336, :])
 
 
-def conv_back_rows(x2, w2, c2, cot, out):
-    @pl.loop(0, HROWS)
+def conv_back_rows(x2, w2, c2, cot, out, lo, hi):
+    @pl.loop(lo, hi)
     def _(h):
         conv_row(x2, w2, c2, h, True)
         for half in range(2):
@@ -165,6 +165,7 @@
 
 
 MESH = pl.DeviceIdType.MESH
+FIRST = 160
 PAIRS = [(i, j) for i in range(BLK // 128) for j in range(i, BLK // 128)]
 
 
@@ -198,8 +199,8 @@
 def block_kernel(
     n, img_hbm, cot_hbm, dw, gain, up_in, down_in, owner,
     mixed_hbm, out_hbm, ag,
-    x2, w2, c2, xhat, rstd, lhs, rhs, up, down, slope, wide, dwb, flat, p, a0, q, a1, gfull, m, c1, img, cot, mixed, out,
-    dws, dwr, ups, upr, downs, downr, a0s, a0r, a1s, a1r, gs, gr, cs, cr, ds, dr, es, er, ios,
+    x2, w2, c2, xhat, rstd, lhs, rhs, up, down, slope, wide, dwb, flat, p, a0, q, ya, qa, za, zb, qb, yb, gfull, m, c1, img, cot, mixed, out,
+    dws, dwr, ups, upr, downs, downr, a0s, a0r, yas, yar, zas, zar, zbs, zbr, ybs, ybr, gs, gr, cs, cr, ds, dr, es, er, ios,
 ):
     img_copy = pltpu.make_async_copy(img_hbm, img, ios.at[0])
     cot_copy = pltpu.make_async_copy(cot_hbm, cot, ios.at[1])
@@ -425,18 +426,51 @@
     scale = (2 * n * PIX) ** -0.5
 
     def slot(i):
-        return lax.rem(pair + 1 + i, n)
+        k, same = lax.rem(i, 4), lax.div(i, 4)
+        return 2 * lax.rem(zpos + k + 1, 4) + ypos + (1 - same) * (1 - 2 * ypos)
+
+    def along(k):
+        return 4 * lax.rem(zpos + k + 1, 4) + 2 * ypos + core
+
+    first, rest = pl.ds(0, FIRST), pl.ds(FIRST, half - FIRST)
 
     def a0_copy(i):
         return dma(p.at[i, other], a0.at[i], a0s.at[i], a0r.at[i], g, sib)
 
-    def a1_copy(i):
-        return dma(q.at[i], a1.at[i], a1s.at[i], a1r.at[i], g, 2 * slot(i) + core)
+    def ya_copy(k):
+        return dma(q.at[k, first], ya.at[k], yas.at[k], yar.at[k], g, across)
+
+    def za_copy(k):
+        return dma(qa.at[k], za.at[k], zas.at[k], zar.at[k], g, along(k))
+
+    def zb_copy(i):
+        return dma(q.at[i, rest], zb.at[i], zbs.at[i], zbr.at[i], g, along(lax.rem(i, 4)))
+
+    yb_copy = dma(qb, yb, ybs, ybr, g, across)
 
     def pass_on(i):
         a0_copy(i).wait_recv()
         q[i] = (p[i, own].astype(F32) + a0[i].astype(F32)).astype(BF16)
-        a1_copy(i).start()
+
+        @pl.when(lax.rem(i, 4) < 3)
+        def _():
+            zb_copy(i).start()
+
+        @pl.when(i < 4)
+        def _():
+            ya_copy(i).start()
+
+    def turn_first(k):
+        ya_copy(k).wait_recv()
+        qa[k] = (q[4 + k, first].astype(F32) + ya[k].astype(F32)).astype(BF16)
+        za_copy(k).start()
+
+    def rest_sum(base):
+        acc = q[base + 3, rest].astype(F32)
+        for k in range(3):
+            zb_copy(base + k).wait_recv()
+            acc = acc + zb[base + k].astype(F32)
+        return acc
 
     @pl.loop(0, n)
     def _(i):
@@ -451,24 +485,35 @@
     def _(j):
         branch_cols(lhs, down, wide, j)
 
+    a0_copy(n - 1).wait_recv()
+    q[n - 1] = (p[n - 1, own].astype(F32) + a0[n - 1].astype(F32)).astype(BF16)
     mix_rows(img, wide, mixed)
     mixed_copy.start()
+    turn_first(0)
 
     @pl.loop(0, 2)
     def _(j):
         back_u_cols(rhs, up, wide, j)
 
+    turn_first(1)
     norm_back_rows(wide, xhat, rstd, gain)
     fill_back(x2, wide)
-    conv_back_rows(x2, w2, c2, cot, out)
+    turn_first(2)
+    conv_back_rows(x2, w2, c2, cot, out, 0, 4)
+    qb[...] = rest_sum(0).astype(BF16)
+    yb_copy.start()
+    conv_back_rows(x2, w2, c2, cot, out, 4, HROWS)
     out_copy.start()
 
-    a0_copy(n - 1).wait_recv()
-    acc = p[n - 1, own].astype(F32) + a0[n - 1].astype(F32)
-    for i in range(n - 1):
-        a1_copy(i).wait_recv()
-        acc = acc + a1[i].astype(F32)
-    gfull[own] = acc.astype(BF16)
+    acc = rest_sum(4)
+    yb_copy.wait_recv()
+    gfull[pl.ds(pl.multiple_of(core * half + FIRST, 16), half - FIRST)] = (acc + yb[...].astype(F32)).astype(BF16)
+    ya_copy(3).wait_recv()
+    acc = q[n - 1, first].astype(F32) + ya[3].astype(F32)
+    for k in range(3):
+        za_copy(k).wait_recv()
+        acc = acc + za[k].astype(F32)
+    gfull[pl.ds(pl.multiple_of(core * half, 16), FIRST)] = acc.astype(BF16)
     g_copy = dma(gfull.at[own], gfull.at[own], gs, gr, g, sib)
     g_copy.start()
     g_copy.wait_recv()
@@ -517,8 +562,14 @@
     for i in range(n):
         a0_copy(i).wait_send()
     for i in range(n - 1):
-        a1_copy(i).wait_send()
         c_copy(i + 1).wait_send()
+    for i in range(4):
+        ya_copy(i).wait_send()
+    for i in range(3):
+        za_copy(i).wait_send()
+        zb_copy(i).wait_send()
+        zb_copy(4 + i).wait_send()
+    yb_copy.wait_send()
     g_copy.wait_send()
 
     @pl.when(pair != g)
@@ -557,8 +608,13 @@
             vmem((64, 32), F32),
             vmem((n, BLK, BLK), BF16),
             vmem((n, half, BLK), BF16),
-            vmem((n - 1, half, BLK), BF16),
-            vmem((n - 1, half, BLK), BF16),
+            vmem((n, half, BLK), BF16),
+            vmem((4, FIRST, BLK), BF16),
+            vmem((3, FIRST, BLK), BF16),
+            vmem((3, FIRST, BLK), BF16),
+            vmem((7, half - FIRST, BLK), BF16),
+            vmem((half - FIRST, BLK), BF16),
+            vmem((half - FIRST, BLK), BF16),
             vmem((BLK, BLK), BF16),
             vmem((n * chunk, 128), BF16),
             vmem((n, chunk, 128), BF16),
@@ -570,7 +626,10 @@
             sem((6, 4)), sem((6, 4)),
             sem((6, 4)), sem((6, 4)),
             sem((n,)), sem((n,)),
-            sem((n - 1,)), sem((n - 1,)),
+            sem((4,)), sem((4,)),
+            sem((3,)), sem((3,)),
+            sem((7,)), sem((7,)),
+            sem, sem,
             sem, sem,
             sem((n,)), sem((n,)),
             sem, sem,

time: 92.2 us -> 84.8 us (0.920)
  Pallas kernels: 91.4 us -> 84 us
    pallas_call x1, Pallas kernels: 88.1 us -> 80.6 us  [local(): pl.pallas_call(functools.partial(block_kernel, n), out_shape=(jax.ShapeDt...]
where the time goes in v5:
time: 84.8 us; the launch traced here: 84.6 us
  Pallas kernels  84 us (99%)
    pallas_call x1, Pallas kernels, local(): pl.pallas_call(functools.partial(block_kernel, n), out_shape=(jax.ShapeDt...  80.6 us
    pallas_call x1, Pallas kernels, local(): pl.pallas_call(finish_kernel, out_shape=(jax.ShapeDtypeStruct((ROWS, COLS...  3.32 us

profile of v5, /device:TPU:1, one launch (start us, length us, event | category | flops | bytes accessed | tf_op | source)
XLA Modules:
  0.0 84.6 jit_solution(4437658755930622084)
XLA Ops:
  0.6 80.6 %shard_map.94 = (bf16[28,28,512]{2,1,0:T(8,128)(2,1)}, bf16[28,28,512]{2,1,0:T(8,128)(2,1)}, bf16[2,1280,128]{2,1,0:T(8,128)(2,1)}) custom-call(bf16[28,28,512]{2,1,0:T(8,128)(2,1)} %bitcast.7, bf16[28,28,512]{2,1,0:T(8,128)(2,1)} %bitcast.8, bf16[32,49]{1,0:T(8,128)(2,1)} %bitcast.9, f32[1,512]{1,0:T(1,128)} %bitcast.10, bf16[32,2048]{1,0:T(8,128)(2,1)} %up_in.1, ...), custom_call_target="tpu_custom_call" | custom-call | tf_op jit(solution)/shard_map/pallas_call | solution.py:586
  81.3 3.3 %shard_map.95 = (bf16[28,28,512]{2,1,0:T(8,128)(2,1)}, bf16[28,28,512]{2,1,0:T(8,128)(2,1)}, f32[2,512,512]{2,1,0:T(8,128)}) custom-call(bf16[28,28,512]{2,1,0:T(8,128)(2,1)} %get-tuple-element.9.mixed_in, bf16[28,28,512]{2,1,0:T(8,128)(2,1)} %get-tuple-element.10.out_in, bf16[2,1280,128]{2,1,0:T(8,128)(2,1)} %get-tuple-element.11.packed_in), custom_call_target="tpu_custom_call" | custom-call | tf_op jit(solution)/shard_map/pallas_call | solution.py:641

commit v6 on v5

--- a/solution.py
+++ b/solution.py
@@ -197,17 +197,15 @@
 
 
 def block_kernel(
-    n, img_hbm, cot_hbm, dw, gain, up_in, down_in, owner,
+    n, img_hbm, cot_hbm, dw_hbm, gain_hbm, up_hbm, down_hbm, owner,
     mixed_hbm, out_hbm, ag,
-    x2, w2, c2, xhat, rstd, lhs, rhs, up, down, slope, wide, dwb, flat, p, a0, q, ya, qa, za, zb, qb, yb, gfull, m, c1, img, cot, mixed, out,
+    x2, w2, c2, xhat, rstd, lhs, rhs, up, down, slope, wide, dwb, flat, p, a0, q, ya, qa, za, zb, qb, yb, gfull, m, c1, img, cot, mixed, out, dw, gain,
     dws, dwr, ups, upr, downs, downr, a0s, a0r, yas, yar, zas, zar, zbs, zbr, ybs, ybr, gs, gr, cs, cr, ds, dr, es, er, ios,
 ):
     img_copy = pltpu.make_async_copy(img_hbm, img, ios.at[0])
     cot_copy = pltpu.make_async_copy(cot_hbm, cot, ios.at[1])
     mixed_copy = pltpu.make_async_copy(mixed, mixed_hbm, ios.at[2])
     out_copy = pltpu.make_async_copy(out, out_hbm, ios.at[3])
-    img_copy.start()
-    cot_copy.start()
     g, s = lax.axis_index("group"), lax.axis_index("shard")
     core, pair = lax.rem(s, 2), lax.div(s, 2)
     sib = s + 1 - 2 * core
@@ -222,13 +220,13 @@
     def peer(i):
         return 2 * lax.rem(pair + i, n) + core
 
-    def gather(mine, place, send, recv):
+    def gather(mine, place, send, recv, base):
         def out_copy(i):
-            return dma(mine, place(s), send.at[0, i], recv.at[0, i], g, peer(i))
+            return dma(mine, place(s), send.at[base, i], recv.at[base, i], g, peer(i))
 
         def on_copy(i):
             j = peer(n - i)
-            return dma(mine if i == 0 else place(j), place(s if i == 0 else j), send.at[1, i], recv.at[1, i], g, sib)
+            return dma(mine if i == 0 else place(j), place(s if i == 0 else j), send.at[base + 1, i], recv.at[base + 1, i], g, sib)
 
         def start():
             on_copy(0).start()
@@ -330,13 +328,27 @@
 
     greet(beyond, across)
 
+    small = [
+        pltpu.make_async_copy(dw_hbm, dw, ios.at[4]),
+        pltpu.make_async_copy(up_hbm, up.at[pl.ds(pl.multiple_of(s * 32, 32), 32)], ios.at[5]),
+        pltpu.make_async_copy(down_hbm, down.at[pl.ds(pl.multiple_of(s * 128, 128), 128)], ios.at[6]),
+        pltpu.make_async_copy(gain_hbm, gain, ios.at[7]),
+    ]
+    for copy in small[:2]:
+        copy.start()
+    img_copy.start()
+    cot_copy.start()
+    for copy in small[2:]:
+        copy.start()
+    small[0].wait()
+
     flat[...] = jnp.zeros_like(flat)
     flat[0:49, :] = dw[...].astype(F32).T
     dwb[s] = jnp.concatenate([flat[16 * t : 16 * t + 16, :] for t in range(4)], axis=1).astype(BF16)
-    up[pl.ds(pl.multiple_of(s * 32, 32), 32), :] = up_in[...]
-    down[pl.ds(pl.multiple_of(s * 128, 128), 128), :] = down_in[...]
     img_copy.wait()
     fill_images(x2, img)
+    for copy in small[1:]:
+        copy.wait()
 
     def up_place(j, h=None):
         return up.at[pl.ds(pl.multiple_of(j * 32 + (h or 0) * 16, 16), 32 if h is None else 16)]
@@ -347,11 +359,12 @@
     up_start, up_far, up_relay_z, up_relay_y, up_arrived, up_finish = spread(up_place, ups, upr)
     down_start, down_far, down_relay_z, down_relay_y, down_arrived, down_finish = spread(down_place, downs, downr)
 
-    def ag_place(j):
-        start = lax.div(j, 2) * chunk
-        return ag.at[lax.rem(j, 2), pl.ds(pl.multiple_of(start, chunk), chunk)]
-
-    ag_start, ag_forward, ag_arrived, ag_finish = gather(ag_place(s), ag_place, es, er)
+    part = chunk // 2
+
+    def ag_place(j, h):
+        return ag.at[lax.rem(j, 2), pl.ds(pl.multiple_of(lax.div(j, 2) * chunk + h * part, part), part)]
+
+    gathers = [gather(ag_place(s, h), lambda j, h=h: ag_place(j, h), es, er, 2 * h) for h in range(2)]
 
     def dw_copy(i):
         return dma(dwb.at[s], dwb.at[s], dws.at[i], dwr.at[i], g, lax.rem(s + i, 2 * n))
@@ -360,6 +373,8 @@
     for i in range(1, 2 * n):
         dw_copy(i).start()
     up_start()
+    up_far()
+    down_start()
     cot_copy.wait()
     flat_rows(cot, rhs)
     for i in range(1, 2 * n):
@@ -380,26 +395,23 @@
         def _(h):
             conv_row(x2, w2, c2, h, False)
 
-    up_far()
-    conv_rows(0, 3)
+    conv_rows(0, 4)
     up_relay_z(1)
     up_relay_z(3)
-    conv_rows(3, 6)
-    down_start()
-    conv_rows(6, 9)
     up_relay_z(2)
-    conv_rows(9, 12)
+    down_far()
+    conv_rows(4, 12)
     up_relay_y(0)
     up_relay_y(1)
     up_relay_y(3)
-    down_far()
     conv_rows(12, HROWS)
+    down_relay_z(1)
+    down_relay_z(3)
     norm_rows(c2, xhat, rstd, 0, 4)
     up_relay_y(2)
-    down_relay_z(1)
-    down_relay_z(3)
     norm_rows(c2, xhat, rstd, 4, 7)
     scale_rows(xhat, gain, lhs)
+    down_relay_z(2)
     up_arrived()
 
     def up_steps(lo, hi):
@@ -407,14 +419,13 @@
         def _(j):
             up_step(lhs, up, slope, j)
 
-    up_steps(0, 2)
-    down_relay_z(2)
-    up_steps(2, 6)
+    up_steps(0, 4)
     down_relay_y(0)
     down_relay_y(1)
     down_relay_y(3)
-    up_steps(6, 8)
+    up_steps(4, 7)
     down_relay_y(2)
+    up_steps(7, 8)
     down_arrived()
 
     @pl.loop(0, 8)
@@ -499,11 +510,10 @@
     norm_back_rows(wide, xhat, rstd, gain)
     fill_back(x2, wide)
     turn_first(2)
-    conv_back_rows(x2, w2, c2, cot, out, 0, 4)
+    conv_back_rows(x2, w2, c2, cot, out, 0, 3)
     qb[...] = rest_sum(0).astype(BF16)
     yb_copy.start()
-    conv_back_rows(x2, w2, c2, cot, out, 4, HROWS)
-    out_copy.start()
+    conv_back_rows(x2, w2, c2, cot, out, 3, 5)
 
     acc = rest_sum(4)
     yb_copy.wait_recv()
@@ -524,45 +534,65 @@
     for b, (i, j) in enumerate(PAIRS):
         m[128 * b : 128 * b + 128, :] = stat[128 * i : 128 * i + 128, 128 * j : 128 * j + 128]
 
-    def m_chunk(j):
-        return pl.ds(pl.multiple_of(j * chunk, chunk), chunk)
-
-    def c_copy(i):
+    def m_part(j, h):
+        return pl.ds(pl.multiple_of(j * chunk + h * part, part), part)
+
+    def c_copy(i, h):
         j = lax.rem(g + i, n)
-        return dma(m.at[m_chunk(j)], c1.at[i], cs.at[i], cr.at[i], j, s)
-
-    for i in range(1, n):
-        c_copy(i).start()
-    acc = m[m_chunk(g), :].astype(F32)
-    for i in range(1, n):
-        c_copy(i).wait_recv()
-        acc = acc + c1[i].astype(F32)
-    c1[0] = acc.astype(BF16)
-    d_copy = dma(c1.at[0], ag_place(mirror[1]), ds, dr, *mirror)
-
-    @pl.when(pair != g)
-    def _():
-        d_copy.start()
-        d_copy.wait_recv()
-
-    @pl.when(pair == g)
-    def _():
-        ag[core, m_chunk(g), :] = c1[0]
-
-    ag_start()
-    ag_forward()
-    ag_arrived()
+        return dma(m.at[m_part(j, h)], c1.at[i, pl.ds(h * part, part)], cs.at[h, i], cr.at[h, i], j, s)
+
+    def d_copy(h):
+        return dma(c1.at[0, pl.ds(h * part, part)], ag_place(mirror[1], h), ds.at[h], dr.at[h], *mirror)
+
+    for h in range(2):
+        for i in range(1, n):
+            c_copy(i, h).start()
+    conv_back_rows(x2, w2, c2, cot, out, 5, 9)
+    for h in range(2):
+        acc = m[m_part(g, h), :].astype(F32)
+        for i in range(1, n):
+            c_copy(i, h).wait_recv()
+            acc = acc + c1[i, part * h : part * h + part, :].astype(F32)
+        total = acc.astype(BF16)
+        c1[0, part * h : part * h + part, :] = total
+
+        @pl.when(pair != g)
+        def _():
+            d_copy(h).start()
+
+        @pl.when(pair == g)
+        def _():
+            ag[core, m_part(g, h), :] = total
+
+    conv_back_rows(x2, w2, c2, cot, out, 9, 11)
+    for h in range(2):
+
+        @pl.when(pair != g)
+        def _():
+            d_copy(h).wait_recv()
+
+        gathers[h][0]()
+
+    conv_back_rows(x2, w2, c2, cot, out, 11, HROWS)
+    out_copy.start()
+    for h in range(2):
+        gathers[h][1]()
+    for h in range(2):
+        gathers[h][2]()
+
     mixed_copy.wait()
     out_copy.wait()
     up_finish()
     down_finish()
-    ag_finish()
+    for h in range(2):
+        gathers[h][3]()
     for i in range(1, 2 * n):
         dw_copy(i).wait_send()
     for i in range(n):
         a0_copy(i).wait_send()
     for i in range(n - 1):
-        c_copy(i + 1).wait_send()
+        c_copy(i + 1, 0).wait_send()
+        c_copy(i + 1, 1).wait_send()
     for i in range(4):
         ya_copy(i).wait_send()
     for i in range(3):
@@ -574,7 +604,8 @@
 
     @pl.when(pair != g)
     def _():
-        d_copy.wait_send()
+        d_copy(0).wait_send()
+        d_copy(1).wait_send()
 
 
 def local(images, cotangent, dw_kernel, norm_gain, w_up, w_down, owner_table):
@@ -590,7 +621,7 @@
             jax.ShapeDtypeStruct((ROWS, COLS, width), BF16),
             jax.ShapeDtypeStruct((2, n * chunk, 128), BF16),
         ),
-        in_specs=[pl.BlockSpec(memory_space=pl.ANY)] * 2 + [pl.BlockSpec(memory_space=vmem)] * 4 + [pl.BlockSpec(memory_space=pltpu.SMEM)],
+        in_specs=[pl.BlockSpec(memory_space=pl.ANY)] * 6 + [pl.BlockSpec(memory_space=pltpu.SMEM)],
         out_specs=[pl.BlockSpec(memory_space=pl.ANY)] * 2 + [pl.BlockSpec(memory_space=vmem)],
         scratch_shapes=[
             vmem((XROWS * XCOLS * 8, 128), F32),
@@ -622,6 +653,8 @@
             vmem((ROWS, COLS, width), BF16),
             vmem((ROWS, COLS, width), BF16),
             vmem((ROWS, COLS, width), BF16),
+            vmem((32, 49), BF16),
+            vmem((1, width), F32),
             sem((2 * n,)), sem((2 * n,)),
             sem((6, 4)), sem((6, 4)),
             sem((6, 4)), sem((6, 4)),
@@ -631,10 +664,10 @@
             sem((7,)), sem((7,)),
             sem, sem,
             sem, sem,
-            sem((n,)), sem((n,)),
-            sem, sem,
             sem((2, n)), sem((2, n)),
-            sem((4,)),
+            sem((2,)), sem((2,)),
+            sem((4, n)), sem((4, n)),
+            sem((8,)),
         ],
         compiler_params=pltpu.CompilerParams(collective_id=0, has_side_effects=True, vmem_limit_bytes=60 * 2**20),
     )(images[0], cotangent[0], dw_kernel.T, norm_gain.reshape(1, width), w_up, w_down, owner_table)

time: 84.8 us -> 83.2 us (0.981)
  Pallas kernels: 84 us -> 82.3 us
    pallas_call x1, Pallas kernels: 80.6 us -> 79 us  [local(): pl.pallas_call(functools.partial(block_kernel, n), out_shape=(jax.ShapeDt...]
where the time goes in v6:
time: 83.2 us; the launch traced here: 83 us
  Pallas kernels  82.3 us (99%)
    pallas_call x1, Pallas kernels, local(): pl.pallas_call(functools.partial(block_kernel, n), out_shape=(jax.ShapeDt...  79 us
    pallas_call x1, Pallas kernels, local(): pl.pallas_call(finish_kernel, out_shape=(jax.ShapeDtypeStruct((ROWS, COLS...  3.32 us

profile of v6, /device:TPU:1, one launch (start us, length us, event | category | flops | bytes accessed | tf_op | source)
XLA Modules:
  0.0 83.0 jit_solution(14716474146614023608)
XLA Ops:
  0.6 79.0 %shard_map.94 = (bf16[28,28,512]{2,1,0:T(8,128)(2,1)}, bf16[28,28,512]{2,1,0:T(8,128)(2,1)}, bf16[2,1280,128]{2,1,0:T(8,128)(2,1)}) custom-call(bf16[28,28,512]{2,1,0:T(8,128)(2,1)} %bitcast.7, bf16[28,28,512]{2,1,0:T(8,128)(2,1)} %bitcast.8, bf16[32,49]{1,0:T(8,128)(2,1)} %bitcast.9, f32[1,512]{1,0:T(1,128)} %bitcast.10, bf16[32,2048]{1,0:T(8,128)(2,1)} %up_hbm.1, ...), custom_call_target="tpu_custom_call" | custom-call | tf_op jit(solution)/shard_map/pallas_call | solution.py:617
  79.7 3.3 %shard_map.95 = (bf16[28,28,512]{2,1,0:T(8,128)(2,1)}, bf16[28,28,512]{2,1,0:T(8,128)(2,1)}, f32[2,512,512]{2,1,0:T(8,128)}) custom-call(bf16[28,28,512]{2,1,0:T(8,128)(2,1)} %get-tuple-element.9.mixed_in, bf16[28,28,512]{2,1,0:T(8,128)(2,1)} %get-tuple-element.10.out_in, bf16[2,1280,128]{2,1,0:T(8,128)(2,1)} %get-tuple-element.11.packed_in), custom_call_target="tpu_custom_call" | custom-call | tf_op jit(solution)/shard_map/pallas_call | solution.py:674

commit v7 on v6

--- a/solution.py
+++ b/solution.py
@@ -165,7 +165,7 @@
 
 
 MESH = pl.DeviceIdType.MESH
-FIRST = 160
+FIRST = 144
 PAIRS = [(i, j) for i in range(BLK // 128) for j in range(i, BLK // 128)]
 
 

time: 83.2 us -> 82.5 us (level)
  no operation moved by 1% of the time
where the time goes in v7:
time: 82.5 us; the launch traced here: 82.4 us
  Pallas kernels  81.7 us (99%)
    pallas_call x1, Pallas kernels, local(): pl.pallas_call(functools.partial(block_kernel, n), out_shape=(jax.ShapeDt...  78.4 us
    pallas_call x1, Pallas kernels, local(): pl.pallas_call(finish_kernel, out_shape=(jax.ShapeDtypeStruct((ROWS, COLS...  3.32 us

profile of v7, /device:TPU:1, one launch (start us, length us, event | category | flops | bytes accessed | tf_op | source)
XLA Modules:
  0.0 82.4 jit_solution(12128316109325958599)
XLA Ops:
  0.6 78.4 %shard_map.94 = (bf16[28,28,512]{2,1,0:T(8,128)(2,1)}, bf16[28,28,512]{2,1,0:T(8,128)(2,1)}, bf16[2,1280,128]{2,1,0:T(8,128)(2,1)}) custom-call(bf16[28,28,512]{2,1,0:T(8,128)(2,1)} %bitcast.7, bf16[28,28,512]{2,1,0:T(8,128)(2,1)} %bitcast.8, bf16[32,49]{1,0:T(8,128)(2,1)} %bitcast.9, f32[1,512]{1,0:T(1,128)} %bitcast.10, bf16[32,2048]{1,0:T(8,128)(2,1)} %up_hbm.1, ...), custom_call_target="tpu_custom_call" | custom-call | tf_op jit(solution)/shard_map/pallas_call | solution.py:617
  79.0 3.3 %shard_map.95 = (bf16[28,28,512]{2,1,0:T(8,128)(2,1)}, bf16[28,28,512]{2,1,0:T(8,128)(2,1)}, f32[2,512,512]{2,1,0:T(8,128)}) custom-call(bf16[28,28,512]{2,1,0:T(8,128)(2,1)} %get-tuple-element.9.mixed_in, bf16[28,28,512]{2,1,0:T(8,128)(2,1)} %get-tuple-element.10.out_in, bf16[2,1280,128]{2,1,0:T(8,128)(2,1)} %get-tuple-element.11.packed_in), custom_call_target="tpu_custom_call" | custom-call | tf_op jit(solution)/shard_map/pallas_call | solution.py:674

commit v8 on v7

--- a/solution.py
+++ b/solution.py
@@ -180,6 +180,9 @@
         stores.append(pltpu.make_async_copy(lines.at[k], dst.at[rows], back.at[k]))
     for copy in loads:
         copy.start()
+    for k in range(8):
+        loads[k].wait()
+        stores[k].start()
     load.wait()
     for side in range(2):
         for b, (i, j) in enumerate(PAIRS):
@@ -189,9 +192,6 @@
                 blocks[side, 128 * j : 128 * j + 128, 128 * i : 128 * i + 128] = part.T
         stores.append(pltpu.make_async_copy(blocks.at[side], stat.at[side], back.at[8 + side]))
         stores[-1].start()
-        for k in range(4 * side, 4 * side + 4):
-            loads[k].wait()
-            stores[k].start()
     for copy in stores:
         copy.wait()
 

time: 82.5 us -> 82.5 us (level)
  no operation moved by 1% of the time
where the time goes in v8:
time: 82.5 us; the launch traced here: 82.3 us
  Pallas kernels  81.7 us (99%)
    pallas_call x1, Pallas kernels, local(): pl.pallas_call(functools.partial(block_kernel, n), out_shape=(jax.ShapeDt...  78.4 us
    pallas_call x1, Pallas kernels, local(): pl.pallas_call(finish_kernel, out_shape=(jax.ShapeDtypeStruct((ROWS, COLS...  3.27 us

profile of v8, /device:TPU:1, one launch (start us, length us, event | category | flops | bytes accessed | tf_op | source)
XLA Modules:
  0.0 82.3 jit_solution(16131946051009731730)
XLA Ops:
  0.6 78.4 %shard_map.94 = (bf16[28,28,512]{2,1,0:T(8,128)(2,1)}, bf16[28,28,512]{2,1,0:T(8,128)(2,1)}, bf16[2,1280,128]{2,1,0:T(8,128)(2,1)}) custom-call(bf16[28,28,512]{2,1,0:T(8,128)(2,1)} %bitcast.7, bf16[28,28,512]{2,1,0:T(8,128)(2,1)} %bitcast.8, bf16[32,49]{1,0:T(8,128)(2,1)} %bitcast.9, f32[1,512]{1,0:T(1,128)} %bitcast.10, bf16[32,2048]{1,0:T(8,128)(2,1)} %up_hbm.1, ...), custom_call_target="tpu_custom_call" | custom-call | tf_op jit(solution)/shard_map/pallas_call | solution.py:617
  79.0 3.3 %shard_map.95 = (bf16[28,28,512]{2,1,0:T(8,128)(2,1)}, bf16[28,28,512]{2,1,0:T(8,128)(2,1)}, f32[2,512,512]{2,1,0:T(8,128)}) custom-call(bf16[28,28,512]{2,1,0:T(8,128)(2,1)} %get-tuple-element.9.mixed_in, bf16[28,28,512]{2,1,0:T(8,128)(2,1)} %get-tuple-element.10.out_in, bf16[2,1280,128]{2,1,0:T(8,128)(2,1)} %get-tuple-element.11.packed_in), custom_call_target="tpu_custom_call" | custom-call | tf_op jit(solution)/shard_map/pallas_call | solution.py:674
